TPU v7x, 32 devices: a whole 2x2x4 slice. The times are simulated.
32 devices in a mesh: dp: 2 (over x), expert: 4 (over z), tensor: 4 (over y, core).
Axes of the slice: x: 2, y: 2, z: 4, core: 2. Of those that a mesh axis runs over, the one named last changes fastest.
Arguments:
- tokens: bfloat16 [1024, 3584], P(('dp', 'expert'), 'tensor'), may hold values from -6 to 6
- cotangent: bfloat16 [1024, 3584], P(('dp', 'expert'), 'tensor'), may hold values from -6 to 6
- routes: int32 [1024, 2], P(('dp', 'expert')), may hold values from 0 to 3, all different within a row; in each aligned block of 128 rows (0 to 127, 128 to 255, ...) at most 80 rows name the same one
- route_weights: float32 [1024, 2], P(('dp', 'expert')), may hold values from 0.2 to 1
- gate_values: bfloat16 [4, 1792, 2560], P('expert', None, 'tensor'), may hold values from -0.125 to 0.125
- up_values: bfloat16 [4, 1792, 2560], P('expert', None, 'tensor'), may hold values from -0.125 to 0.125
- down_values: bfloat16 [4, 1280, 3584], P('expert', 'tensor'), may hold values from -0.15625 to 0.15625
- gate_words: int32 [4, 224, 2560], P('expert', None, 'tensor'), may hold values from 0 to 1295
- up_words: int32 [4, 224, 2560], P('expert', None, 'tensor'), may hold values from 0 to 1295
- down_words: int32 [4, 160, 3584], P('expert', 'tensor'), may hold values from 0 to 1295
- res_gate: bfloat16 [3584, 3072], P(None, ('dp', 'tensor')), may hold values from -0.09375 to 0.09375
- res_up: bfloat16 [3584, 3072], P(None, ('dp', 'tensor')), may hold values from -0.09375 to 0.09375
- res_down: bfloat16 [3584, 3072], P(None, ('dp', 'tensor')), may hold values from -0.109375 to 0.109375
Outputs:
- tokens_grad: bfloat16 [1024, 3584], P(('dp', 'expert'), 'tensor')
- gate_values_grad: bfloat16 [4, 1792, 2560], P('expert', 'dp', 'tensor')
- up_values_grad: bfloat16 [4, 1792, 2560], P('expert', 'dp', 'tensor')
- down_values_grad: bfloat16 [4, 1280, 3584], P('expert', 'tensor', 'dp')
- res_gate_grad: bfloat16 [3584, 3072], P('expert', ('dp', 'tensor'))
- res_up_grad: bfloat16 [3584, 3072], P('expert', ('dp', 'tensor'))
- res_down_grad: bfloat16 [3584, 3072], P('expert', ('dp', 'tensor'))
Inputs may be any that keep to these rules, and one draw needn't show every extreme that they name: `routes`: each row names two different experts. Within the 128 rows of one token group no expert is named more than 80 times, a bound that some block reaches. `gate_words`: each entry is a word of four base-6 digits; digit k of entry [e, j, c] names the kept positions of the group of rows 16 * j + 4 * k to 16 * j + 4 * k + 3 in column c. `up_words`: laid out as gate_words. `down_words`: digit k of entry [e, j, c] names the kept positions of the group of hidden rows 16 * j + 4 * k to 16 * j + 4 * k + 3 in column c.
All inputs are finite; a program needn't handle non-finite values.
Results may differ from a plain program's by a relative error of at most 0.0095.
Values may be sent and summed in bfloat16 or wider, within the bound.
A program may use at most 256 MiB of HBM per device.

v0:
```python
import jax
import jax.numpy as jnp
from jax import lax
from jax.sharding import PartitionSpec as P

powers_six = (1, 6, 36, 216)


def kept_masks(word_rows):
    digits = jnp.stack([word_rows // place_value % 6 for place_value in powers_six], axis=1)
    pattern = digits.reshape((word_rows.shape[0] * 4,) + word_rows.shape[1:])
    past_three = (pattern >= 3).astype(jnp.int32)
    past_five = (pattern >= 5).astype(jnp.int32)
    lead_pos = past_three + past_five
    trail_pos = pattern + 1 - 2 * past_three - past_five
    places = jnp.arange(4, dtype=jnp.int32).reshape(1, 4, 1)
    return (lead_pos[:, None] == places, trail_pos[:, None] == places)


def expand_rows(values, masks):
    lead_hit, trail_hit = masks
    paired = values.reshape((values.shape[0] // 2, 2) + values.shape[1:])
    nothing = jnp.zeros_like(paired[:, 0:1])
    dense = jnp.where(lead_hit, paired[:, 0:1], jnp.where(trail_hit, paired[:, 1:2], nothing))
    return dense.reshape((values.shape[0] * 2,) + values.shape[1:])


def compress_rows(dense_grad, masks):
    lead_hit, trail_hit = masks
    grouped = dense_grad.reshape((dense_grad.shape[0] // 4, 4) + dense_grad.shape[1:])
    nothing = jnp.zeros_like(grouped)
    lead_vals = jnp.sum(jnp.where(lead_hit, grouped, nothing), axis=1)
    trail_vals = jnp.sum(jnp.where(trail_hit, grouped, nothing), axis=1)
    return jnp.stack([lead_vals, trail_vals], axis=1).reshape(
        (dense_grad.shape[0] // 2,) + dense_grad.shape[1:]
    )


def slot_table(route_block, weight_block, experts, capacity):
    row_count = route_block.shape[0]
    flat_routes = route_block.reshape(-1)
    onehot = (flat_routes[:, None] == jnp.arange(experts, dtype=jnp.int32)[None, :]).astype(
        jnp.int32
    )
    before = jnp.cumsum(onehot, axis=0, dtype=jnp.int32) - onehot
    rank_in = jnp.sum(before * onehot, axis=1, dtype=jnp.int32)
    slot_index = flat_routes * capacity + rank_in
    owners = jnp.arange(2 * row_count, dtype=jnp.int32) // 2
    sources = jnp.full((experts * capacity,), row_count, jnp.int32).at[slot_index].set(owners)
    scales = (
        jnp.zeros((experts * capacity,), jnp.float32).at[slot_index].set(weight_block.reshape(-1))
    )
    return (slot_index, sources, scales)


def build_rows(row_block, cot_block, sources, scales, experts, capacity):
    row_width = row_block.shape[1]
    filler = jnp.zeros((1, row_width), row_block.dtype)
    padded_rows = jnp.concatenate([row_block, filler], axis=0)
    padded_cot = jnp.concatenate([cot_block, filler], axis=0)
    sent_rows = padded_rows[sources].reshape(experts, capacity, row_width)
    weighted = (padded_cot[sources].astype(jnp.float32) * scales[:, None]).astype(jnp.bfloat16)
    return (sent_rows, weighted.reshape(experts, capacity, row_width))


def swiglu_back(row_block, cotangent_rows, w_gate, w_up, w_down, down_spec):
    gate_pre = jnp.dot(row_block, w_gate, preferred_element_type=jnp.float32)
    up_pre = jnp.dot(row_block, w_up, preferred_element_type=jnp.float32)
    active = jax.nn.silu(gate_pre)
    hidden = (active * up_pre).astype(jnp.bfloat16)
    if down_spec == "hidden_first":
        hid_grad = jnp.einsum(
            "sd,hd->sh", cotangent_rows, w_down, preferred_element_type=jnp.float32
        )
    else:
        hid_grad = jnp.einsum(
            "sd,dh->sh", cotangent_rows, w_down, preferred_element_type=jnp.float32
        )
    sigmoid_gate = jax.nn.sigmoid(gate_pre)
    gate_grad = (hid_grad * up_pre * sigmoid_gate * (1.0 + gate_pre * (1.0 - sigmoid_gate))).astype(
        jnp.bfloat16
    )
    up_grad = (hid_grad * active).astype(jnp.bfloat16)
    row_grad = jnp.einsum(
        "sh,dh->sd", gate_grad, w_gate, preferred_element_type=jnp.float32
    ) + jnp.einsum("sh,dh->sd", up_grad, w_up, preferred_element_type=jnp.float32)
    gate_term = jnp.einsum("sd,sh->dh", row_block, gate_grad, preferred_element_type=jnp.float32)
    up_term = jnp.einsum("sd,sh->dh", row_block, up_grad, preferred_element_type=jnp.float32)
    if down_spec == "hidden_first":
        down_term = jnp.einsum(
            "sh,sd->hd", hidden, cotangent_rows, preferred_element_type=jnp.float32
        )
    else:
        down_term = jnp.einsum(
            "sd,sh->dh", cotangent_rows, hidden, preferred_element_type=jnp.float32
        )
    return (row_grad, gate_term, up_term, down_term)


def gather_pairs(returned, slot_index):
    flat_rows = returned.reshape(-1, returned.shape[2])
    picked = flat_rows[slot_index].reshape(-1, 2, returned.shape[2])
    return picked[:, 0] + picked[:, 1]


def split_blocks(row_grad, dp_count, tensor_count):
    rows = row_grad.shape[0] // dp_count
    blocks = row_grad.reshape(dp_count, rows, tensor_count, -1).transpose(0, 2, 1, 3)
    return blocks.reshape(dp_count * tensor_count, rows, -1)


def shards(
    tokens,
    cotangent,
    routes,
    route_weights,
    gate_values,
    up_values,
    down_values,
    gate_words,
    up_words,
    down_words,
    res_gate,
    res_up,
    res_down,
):
    experts = lax.axis_size("expert")
    dp_count = lax.axis_size("dp")
    tensor_count = lax.axis_size("tensor")
    tok_count = tokens.shape[0]
    capacity = 5 * tok_count // (2 * experts)
    slot_index, sources, scales = slot_table(routes, route_weights, experts, capacity)
    whole_tok, whole_cot = (
        lax.all_gather(tokens, "tensor", axis=1, tiled=True),
        lax.all_gather(cotangent, "tensor", axis=1, tiled=True),
    )
    send_tok, send_cot = build_rows(whole_tok, whole_cot, sources, scales, experts, capacity)
    slot_tok, slot_cot = (
        lax.all_to_all(send_tok, "expert", split_axis=0, concat_axis=0, tiled=True),
        lax.all_to_all(send_cot, "expert", split_axis=0, concat_axis=0, tiled=True),
    )
    row_width = whole_tok.shape[1]
    slot_tok = slot_tok.reshape(experts * capacity, row_width)
    slot_cot = slot_cot.reshape(experts * capacity, row_width)
    gate_masks = kept_masks(gate_words[0])
    up_masks = kept_masks(up_words[0])
    down_masks = kept_masks(down_words[0])
    gate_dense = expand_rows(gate_values[0], gate_masks)
    up_dense = expand_rows(up_values[0], up_masks)
    down_dense = expand_rows(down_values[0], down_masks)
    slot_grad, gate_term, up_term, down_term = swiglu_back(
        slot_tok, slot_cot, gate_dense, up_dense, down_dense, "hidden_first"
    )
    gate_share, up_share = (
        lax.psum_scatter(
            compress_rows(gate_term, gate_masks)[None].astype(jnp.bfloat16),
            "dp",
            scatter_dimension=1,
            tiled=True,
        ).astype(jnp.float32),
        lax.psum_scatter(
            compress_rows(up_term, up_masks)[None].astype(jnp.bfloat16),
            "dp",
            scatter_dimension=1,
            tiled=True,
        ).astype(jnp.float32),
    )
    down_share = lax.psum_scatter(
        compress_rows(down_term, down_masks)[None].astype(jnp.bfloat16),
        "dp",
        scatter_dimension=2,
        tiled=True,
    )
    pair_tok, pair_cot = (
        lax.all_gather(whole_tok, "dp", axis=0, tiled=True),
        lax.all_gather(whole_cot, "dp", axis=0, tiled=True),
    )
    res_grad, res_gate_term, res_up_term, res_down_term = swiglu_back(
        pair_tok, pair_cot, res_gate, res_up, res_down, "model_first"
    )
    moe_rows = slot_grad.reshape(experts, capacity, row_width)
    shares = lax.psum_scatter(moe_rows, "tensor", scatter_dimension=2, tiled=True)
    returned = lax.all_to_all(shares, "expert", split_axis=0, concat_axis=0, tiled=True)
    res_share = lax.psum_scatter(
        split_blocks(res_grad, dp_count, tensor_count),
        ("dp", "tensor"),
        scatter_dimension=0,
        tiled=True,
    )
    combined = res_share[0] + gather_pairs(returned, slot_index)
    res_gate_sum, res_up_sum, res_down_sum = (
        lax.psum_scatter(
            res_gate_term.astype(jnp.bfloat16), "expert", scatter_dimension=0, tiled=True
        ).astype(jnp.float32),
        lax.psum_scatter(
            res_up_term.astype(jnp.bfloat16), "expert", scatter_dimension=0, tiled=True
        ).astype(jnp.float32),
        lax.psum_scatter(
            res_down_term.astype(jnp.bfloat16), "expert", scatter_dimension=0, tiled=True
        ).astype(jnp.float32),
    )
    return (
        combined.astype(jnp.bfloat16),
        gate_share.astype(jnp.bfloat16),
        up_share.astype(jnp.bfloat16),
        down_share,
        res_gate_sum.astype(jnp.bfloat16),
        res_up_sum.astype(jnp.bfloat16),
        res_down_sum.astype(jnp.bfloat16),
    )


def solution(mesh):
    in_specs = (
        P(("dp", "expert"), "tensor"),
        P(("dp", "expert"), "tensor"),
        P(("dp", "expert"), None),
        P(("dp", "expert"), None),
        P("expert", None, "tensor"),
        P("expert", None, "tensor"),
        P("expert", "tensor", None),
        P("expert", None, "tensor"),
        P("expert", None, "tensor"),
        P("expert", "tensor", None),
        P(None, ("dp", "tensor")),
        P(None, ("dp", "tensor")),
        P(None, ("dp", "tensor")),
    )
    out_specs = (
        P(("dp", "expert"), "tensor"),
        P("expert", "dp", "tensor"),
        P("expert", "dp", "tensor"),
        P("expert", "tensor", "dp"),
        P("expert", ("dp", "tensor")),
        P("expert", ("dp", "tensor")),
        P("expert", ("dp", "tensor")),
    )
    return jax.shard_map(shards, mesh=mesh, in_specs=in_specs, out_specs=out_specs, check_vma=False)
```

profile of v0, /device:TPU:0, one launch (start us, length us, event | category | flops | bytes accessed | tf_op | source)
XLA Modules:
  0.0 794.4 jit_solution(5993157495821664656)
XLA Ops:
  8.1 12.6 %all_gather.14 = bf16[128,3584]{1,0:T(8,128)(2,1)} all-gather(bf16[128,896]{1,0:T(8,128)(2,1)} %param.13), channel_id=1, replica_groups=mesh['dp'=2,'expert'=4,'tensor'=4] {'tensor'}, dimensions={1}, use_global_device_ids=true | all-gather | bytes 1146880 | tf_op jit(solution)/shard_map/all_gather | solution.py:134
  27.3 8.9 %gather_fusion.1 = bf16[320,3584]{1,0:T(8,128)(2,1)} fusion(bf16[129,3584]{1,0:T(8,128)(2,1)} %concatenate.7, s32[1024]{0:T(1024)S(1)} %pad_clamp_fusion.1), kind=kCustom, calls=%fused_computation.1 | custom fusion | bytes 4588800 | tf_op jit(solution)/shard_map/gather | solution.py:61
  41.2 10.2 %all_gather.12 = bf16[128,3584]{1,0:T(8,128)(2,1)} all-gather(bf16[128,896]{1,0:T(8,128)(2,1)S(1)} %copy-done.22), channel_id=1, replica_groups=mesh['dp'=2,'expert'=4,'tensor'=4] {'tensor'}, dimensions={1}, use_global_device_ids=true | all-gather | bytes 1146880 | tf_op jit(solution)/shard_map/all_gather | solution.py:135
  94.3 8.4 %select_n.394 = bf16[3584,640]{1,0:T(8,128)(2,1)} reshape(bf16[896,4,640]{2,1,0:T(4,128)(2,1)} %copy.139) | data formatting | bytes 9175040 | tf_op jit(solution)/shard_map/jit(_where)/select_n | solution.py:24
  126.8 6.3 fusion.67
  143.5 8.4 %select_n.384 = bf16[3584,640]{1,0:T(8,128)(2,1)} reshape(bf16[896,4,640]{2,1,0:T(4,128)(2,1)} %copy.134) | data formatting | bytes 9175040 | tf_op jit(solution)/shard_map/jit(_where)/select_n | solution.py:24
  174.2 8.8 %gather_fusion = bf16[320,3584]{1,0:T(8,128)(2,1)} fusion(bf16[129,3584]{1,0:T(8,128)(2,1)} %concatenate.6, s32[1024]{0:T(1024)S(1)} %copy-done.24), kind=kCustom, calls=%fused_computation | custom fusion | bytes 4588800 | tf_op jit(solution)/shard_map/gather | solution.py:62
  209.0 7.2 select_n.374
  216.2 6.8 eq.225.clone
  223.0 11.5 %eq.231 = s32[3584,640]{1,0:T(8,128)} reshape(s32[896,4,640]{2,1,0:T(4,128)} %eq.225.clone) | data formatting | bytes 18350080 | tf_op jit(solution)/shard_map/eq | solution.py:17
  234.5 6.9 eq.228.clone
  241.3 11.5 %eq.236 = s32[3584,640]{1,0:T(8,128)} reshape(s32[896,4,640]{2,1,0:T(4,128)} %eq.228.clone) | data formatting | bytes 18350080 | tf_op jit(solution)/shard_map/eq | solution.py:17
  257.3 8.5 %broadcast_in_dim.126 = bf16[3584,640]{1,0:T(8,128)(2,1)} reshape(bf16[896,4,640]{2,1,0:T(4,128)(2,1)} %broadcast_in_dim.123.clone) | data formatting | bytes 9175040 | tf_op jit(solution)/shard_map/jit(_where)/broadcast_in_dim | solution.py:24
  270.4 8.3 %broadcast_in_dim.127 = bf16[3584,640]{1,0:T(8,128)(2,1)} reshape(bf16[896,4,640]{2,1,0:T(4,128)(2,1)} %broadcast_in_dim.125.clone) | data formatting | bytes 9175040 | tf_op jit(solution)/shard_map/jit(_where)/broadcast_in_dim | solution.py:24
  279.1 6.7 eq.219.clone
  285.8 11.5 %eq.238 = s32[3584,640]{1,0:T(8,128)} reshape(s32[896,4,640]{2,1,0:T(4,128)} %eq.219.clone) | data formatting | bytes 18350080 | tf_op jit(solution)/shard_map/eq | solution.py:17
  297.2 6.6 eq.222.clone
  303.9 11.4 %eq.240 = s32[3584,640]{1,0:T(8,128)} reshape(s32[896,4,640]{2,1,0:T(4,128)} %eq.222.clone) | data formatting | bytes 18350080 | tf_op jit(solution)/shard_map/eq | solution.py:17
  319.8 8.3 %broadcast_in_dim.129 = bf16[3584,640]{1,0:T(8,128)(2,1)} reshape(bf16[896,4,640]{2,1,0:T(4,128)(2,1)} %broadcast_in_dim.118.clone) | data formatting | bytes 9175040 | tf_op jit(solution)/shard_map/jit(_where)/broadcast_in_dim | solution.py:24
  332.7 8.8 %broadcast_in_dim.130 = bf16[3584,640]{1,0:T(8,128)(2,1)} reshape(bf16[896,4,640]{2,1,0:T(4,128)(2,1)} %broadcast_in_dim.120.clone) | data formatting | bytes 9175040 | tf_op jit(solution)/shard_map/jit(_where)/broadcast_in_dim | solution.py:24
  357.8 13.4 %fusion.9 = f32[320,3584]{1,0:T(8,128)} fusion(bf16[320,640]{1,0:T(8,128)(2,1)S(1)} %get-tuple-element.54, bf16[3584,640]{1,0:T(8,128)(2,1)} %broadcast_in_dim.126, s32[3584,640]{1,0:T(8,128)} %eq.231, bf16[3584,640]{1,0:T(8,128)(2,1)} %broadcast_in_dim.127, s32[3584,640]{1,0:T(8,128)} %eq.236, s32[3584]{0:T(1024)S(1)} %eq.233), kind=kOutput, calls=%fused_computation.35 | convolution fusion | flops 1477181440 | bytes 32536576 | tf_op jit(solution)/shard_map/sh,dh->sd/dot_general | solution.py:84
  371.2 11.8 %convolution_add_fusion = f32[320,3584]{1,0:T(8,128)} fusion(f32[320,3584]{1,0:T(8,128)} %fusion.9, bf16[320,640]{1,0:T(8,128)(2,1)S(1)} %get-tuple-element.53, bf16[3584,640]{1,0:T(8,128)(2,1)} %broadcast_in_dim.129, s32[3584,640]{1,0:T(8,128)S(1)} %bitcast.283, bf16[3584,640]{1,0:T(8,128)(2,1)} %broadcast_in_dim.130, s32[3584,640]{1,0:T(8,128)} %eq.240, ...), kind=kOutput, calls=%fused_computation.30 | convolution fusion | flops 1478328320 | bytes 37124096 | tf_op jit(solution)/shard_map/sh,dh->sd/dot_general | solution.py:86
  444.6 6.0 copy.151
  450.6 7.3 select_reduce_fusion.3
  468.7 7.3 select_reduce_fusion.5
  488.5 6.9 select_reduce_fusion.1
  508.7 54.4 %all-to-all-done.2 = f32[4,80,896]{2,1,0:T(8,128)} async-done(((f32[4,80,896]{2,1,0:T(8,128)}), f32[4,80,896]{2,1,0:T(8,128)}, u32[]{:S(2)}, u32[]{:S(2)}) %all-to-all-start.2) | async-done | bytes 1146912 | tf_op jit(solution)/shard_map/all_to_all | solution.py:183
  574.4 45.8 %reduce-scatter.27.cloned.1.call-done = bf16[896,384]{1,0:T(8,128)(2,1)} async-done(((bf16[3584,384]{1,0:T(8,128)(2,1)}), bf16[896,384]{1,0:T(8,128)(2,1)}) %reduce-scatter.27.cloned.1.call-update) | async-done | bytes 688144
  620.2 56.8 %reduce-scatter.29.cloned.1.call-done = bf16[896,384]{1,0:T(8,128)(2,1)} async-done(((bf16[3584,384]{1,0:T(8,128)(2,1)}), bf16[896,384]{1,0:T(8,128)(2,1)}) %reduce-scatter.29.cloned.1.call-update) | async-done | bytes 688144
  677.0 36.4 %reduce-scatter.21.cloned.1.call-done = bf16[1,896,640]{2,1,0:T(8,128)(2,1)} async-done(((bf16[1,1792,640]{2,1,0:T(8,128)(2,1)}), bf16[1,896,640]{2,1,0:T(8,128)(2,1)}) %reduce-scatter.21.cloned.1.call-update) | async-done | bytes 1146896 | tf_op jit(solution)/shard_map/reduce_scatter | solution.py:161
  713.4 36.7 %reduce-scatter.19.cloned.1.call-done = bf16[1,896,640]{2,1,0:T(8,128)(2,1)} async-done(((bf16[1,1792,640]{2,1,0:T(8,128)(2,1)}), bf16[1,896,640]{2,1,0:T(8,128)(2,1)}) %reduce-scatter.19.cloned.1.call-update) | async-done | bytes 1146896 | tf_op jit(solution)/shard_map/reduce_scatter | solution.py:155
  750.1 36.6 %reduce-scatter.23.cloned.1.call-done = bf16[1,320,1792]{2,1,0:T(8,128)(2,1)} async-done(((bf16[1,320,3584]{2,1,0:T(8,128)(2,1)}), bf16[1,320,1792]{2,1,0:T(8,128)(2,1)}) %reduce-scatter.23.cloned.1.call-update) | async-done | bytes 1146896 | tf_op jit(solution)/shard_map/reduce_scatter | solution.py:168
  (201 shorter events, 281.2 us)
Async XLA Ops:
  8.0 378.9 %copy-start = (bf16[3584,384]{1,0:T(8,128)(2,1)S(1)}, bf16[3584,384]{1,0:T(8,128)(2,1)}, u32[]{:S(2)}) copy-start(bf16[3584,384]{1,0:T(8,128)(2,1)} %param.23) | copy-start | bytes 8257540
  8.0 15.3 %copy-start.25 = (s32[128,2]{0,1:T(2,128)S(1)}, s32[128,2]{0,1:T(2,128)}, u32[]{:S(2)}) copy-start(s32[128,2]{0,1:T(2,128)} %param.15) | copy-start | bytes 3076
  8.0 375.3 %all-gather.5.cloned.1.call-start = ((), (), s32[]{:S(2)}) async-start(), calls=%async_computation.12 | async-start | bytes 2752512 | tf_op jit(solution)/shard_map/all_gather | solution.py:175
  25.8 10.3 %copy-start.26 = (s32[256,1]{0,1:T(1,128)}, s32[256,1]{0,1:T(1,128)S(1)}, u32[]{:S(2)}) copy-start(s32[256,1]{0,1:T(1,128)S(1)} %compare_select_fusion.8) | copy-start | bytes 3076
  27.3 8.9 %copy-start.23 = (s32[1024]{0:T(1024)}, s32[1024]{0:T(1024)S(1)}, u32[]{:S(2)}) copy-start(s32[1024]{0:T(1024)S(1)} %pad_clamp_fusion.1) | copy-start | bytes 12292
  36.2 5.0 copy-start.22
  36.2 156.9 %all-to-all-start.1 = ((bf16[4,80,3584]{2,1,0:T(8,128)(2,1)}), bf16[4,80,3584]{2,1,0:T(8,128)(2,1)}, u32[]{:S(2)}, u32[]{:S(2)}) async-start(bf16[4,80,3584]{2,1,0:T(8,128)(2,1)} %bitcast.287), calls=%async_computation.2 | async-start | bytes 4587520 | tf_op jit(solution)/shard_map/all_to_all | solution.py:139
  41.2 12.5 %copy-start.15 = (s32[1,224,640]{2,1,0:T(8,128)S(1)}, s32[1,224,640]{2,1,0:T(8,128)}, u32[]{:S(2)}) copy-start(s32[1,224,640]{2,1,0:T(8,128)} %param.20) | copy-start | bytes 1720324
  41.2 347.6 %all-gather.3.cloned.1.call-start = ((), (), s32[]{:S(2)}) async-start(), calls=%async_computation.11 | async-start | bytes 2752512 | tf_op jit(solution)/shard_map/all_gather | solution.py:176
  84.1 4.6 copy-start.6
  94.3 8.4 %copy-start.16 = (s32[1,224,640]{2,1,0:T(8,128)S(1)}, s32[1,224,640]{2,1,0:T(8,128)}, u32[]{:S(2)}) copy-start(s32[1,224,640]{2,1,0:T(8,128)} %param.21) | copy-start | bytes 1720324
  143.5 8.4 %copy-start.17 = (s32[1,40,3584]{2,1,0:T(8,128)S(1)}, s32[1,40,3584]{2,1,0:T(8,128)}, u32[]{:S(2)}) copy-start(s32[1,40,3584]{2,1,0:T(8,128)} %param.22) | copy-start | bytes 1720324
  174.2 8.8 %copy-start.28 = (f32[128,2]{0,1:T(2,128)S(1)}, f32[128,2]{0,1:T(2,128)}, u32[]{:S(2)}) copy-start(f32[128,2]{0,1:T(2,128)} %param.16) | copy-start | bytes 3076
  193.1 159.0 %all-to-all-start = ((bf16[4,80,3584]{2,1,0:T(8,128)(2,1)}), bf16[4,80,3584]{2,1,0:T(8,128)(2,1)}, u32[]{:S(2)}, u32[]{:S(2)}) async-start(bf16[4,80,3584]{2,1,0:T(8,128)(2,1)} %fusion.10), calls=%async_computation.1 | async-start | bytes 4587520 | tf_op jit(solution)/shard_map/all_to_all | solution.py:140
  198.0 305.7 %reduce-scatter.17.cloned.1.call-start = ((), (), s32[]{:S(2)}) async-start(), calls=%async_computation.14 | async-start | bytes 5734400 | tf_op jit(solution)/shard_map/reduce_scatter | solution.py:182
  332.7 14.8 %slice-start.3 = ((s8[4587520]{0:T(1024)(128)(4,1)}), s8[393216]{0:T(1024)(128)(4,1)S(1)}, s32[]{:S(2)}) async-start(s8[4587520]{0:T(1024)(128)(4,1)} %bitcast.289), calls=%async_computation.24 | async-start | bytes 786432
  341.5 6.0 slice-start.4
  352.1 19.1 %slice-start = ((s8[9175040]{0:T(1024)(128)(4,1)}), s8[4194304]{0:T(1024)(128)(4,1)S(1)}, s32[]{:S(2)}) async-start(s8[9175040]{0:T(1024)(128)(4,1)} %bitcast.282), calls=%async_computation.21 | async-start | bytes 8388608
  352.1 19.1 %slice-start.1 = ((s8[9175040]{0:T(1024)(128)(4,1)}), s8[4194304]{0:T(1024)(128)(4,1)S(1)}, s32[]{:S(2)}) async-start(s8[9175040]{0:T(1024)(128)(4,1)} %bitcast.282), calls=%async_computation.22 | async-start | bytes 8388608
  357.8 13.5 %copy-start.18 = (bf16[320,640]{1,0:T(8,128)(2,1)}, bf16[320,640]{1,0:T(8,128)(2,1)S(1)}, u32[]{:S(2)}) copy-start(bf16[320,640]{1,0:T(8,128)(2,1)S(1)} %get-tuple-element.54) | copy-start | bytes 1228804
  357.8 13.4 %copy-start.20 = (bf16[320,640]{1,0:T(8,128)(2,1)}, bf16[320,640]{1,0:T(8,128)(2,1)S(1)}, u32[]{:S(2)}) copy-start(bf16[320,640]{1,0:T(8,128)(2,1)S(1)} %get-tuple-element.53) | copy-start | bytes 1228804
  357.8 13.5 %slice-start.2 = ((s8[9175040]{0:T(1024)(128)(4,1)}), s8[786432]{0:T(1024)(128)(4,1)S(1)}, s32[]{:S(2)}) async-start(s8[9175040]{0:T(1024)(128)(4,1)} %bitcast.282), calls=%async_computation.23 | async-start | bytes 1572864
  383.1 189.4 %reduce-scatter.15.cloned.1.call-start = ((), (), s32[]{:S(2)}) async-start(), calls=%async_computation.13 | async-start | bytes 4128768 | tf_op jit(solution)/shard_map/reduce_scatter | solution.py:184
  407.6 166.8 %reduce-scatter.25.cloned.1.call-start = ((), (), s32[]{:S(2)}) async-start(), calls=%async_computation.18 | async-start | bytes 3440640
  416.2 204.0 %reduce-scatter.27.cloned.1.call-start = ((), (), s32[]{:S(2)}) async-start(), calls=%async_computation.19 | async-start | bytes 3440640
  424.7 252.3 %reduce-scatter.29.cloned.1.call-start = ((), (), s32[]{:S(2)}) async-start(), calls=%async_computation.20 | async-start | bytes 3440640
  434.2 279.2 %reduce-scatter.21.cloned.1.call-start = ((), (), s32[]{:S(2)}) async-start(), calls=%async_computation.16 | async-start | bytes 3440640 | tf_op jit(solution)/shard_map/reduce_scatter | solution.py:161
  444.6 6.0 copy-start.21
  467.8 282.4 %reduce-scatter.19.cloned.1.call-start = ((), (), s32[]{:S(2)}) async-start(), calls=%async_computation.15 | async-start | bytes 3440640 | tf_op jit(solution)/shard_map/reduce_scatter | solution.py:155
  486.0 300.7 %reduce-scatter.23.cloned.1.call-start = ((), (), s32[]{:S(2)}) async-start(), calls=%async_computation.17 | async-start | bytes 3440640 | tf_op jit(solution)/shard_map/reduce_scatter | solution.py:168
  503.6 5.1 copy-start.27
  503.7 59.4 %all-to-all-start.2 = ((f32[4,80,896]{2,1,0:T(8,128)}), f32[4,80,896]{2,1,0:T(8,128)}, u32[]{:S(2)}, u32[]{:S(2)}) async-start(f32[4,80,896]{2,1,0:T(8,128)} %reduce-scatter.17.cloned.1.call-done), calls=%async_computation.4 | async-start | bytes 2293760 | tf_op jit(solution)/shard_map/all_to_all | solution.py:183
  (16 other events, 47.8 us)
Sparse Core Ops, SparseCore 0:
  20.8 30.4 all-gather.4
  52.9 30.1 all-gather.2
Sparse Core Ops, SparseCore 1:
  383.1 47.8 reduce-scatter.16
  434.8 48.6 reduce-scatter.14
  486.2 72.3 reduce-scatter.24
  561.4 58.7 reduce-scatter.26
  623.1 53.8 reduce-scatter.28
  679.8 33.5 reduce-scatter.20
  716.2 33.9 reduce-scatter.18
  752.8 33.9 reduce-scatter.22
where the time goes:
time: 804 us; the launch traced here: 794 us
  local copies, waits for them, and re-layouts  359 us (45%)
  waiting for transfers between devices  267 us (33%)
  matrix products  87.6 us (11%)
  other arithmetic  25.1 us (3%)
  blocking collectives  22.8 us (3%)
  starting transfers between devices  16.3 us (2%)
  between operations  16.3 us (2%)
    unnamed x13, waiting for transfers between devices  103 us
    eq x10, local copies, waits for them, and re-layouts, kept_masks(): return (lead_pos[:, None] == places, trail_pos[:, None] == places)  73.1 us
    all_to_all x1, waiting for transfers between devices, shards(): lax.all_to_all(shares, 'expert', split_axis=0, concat_axis=0, tiled=True)  54.4 us
    select_n x6, local copies, waits for them, and re-layouts, expand_rows(): jnp.where(lead_hit, paired[:, 0:1], jnp.where(trail_hit, paired[:, 1:2],...  40.9 us
    reduce_scatter x1, waiting for transfers between devices, shards(): lax.psum_scatter(compress_rows(gate_term, gate_masks)[None].astype(jnp.bf...  36.7 us
    reduce_scatter x1, waiting for transfers between devices, shards(): lax.psum_scatter(compress_rows(down_term, down_masks)[None].astype(jnp.bf...  36.6 us
    reduce_scatter x1, waiting for transfers between devices, shards(): lax.psum_scatter(compress_rows(up_term, up_masks)[None].astype(jnp.bfloat...  36.4 us
    broadcast_in_dim x7, local copies, waits for them, and re-layouts, expand_rows(): jnp.where(trail_hit, paired[:, 1:2], nothing)  29.8 us
  transfers between devices with their start and end apart: 13, of which 6 were waited for; matrix products, arithmetic and copies ran while one was open for 58% of the time, Pallas kernels for 0%

commit v1 on v0

v1 whole, which is shorter than its diff:
```python
import functools

import jax
import jax.numpy as jnp
from jax import lax
from jax.experimental import pallas as pl
from jax.experimental.pallas import tpu as pltpu
from jax.sharding import PartitionSpec as P

VMEM_BYTES = 56 * 1024 * 1024


def call(body, **settings):
    return pl.pallas_call(
        body,
        compiler_params=pltpu.CompilerParams(vmem_limit_bytes=VMEM_BYTES),
        **settings,
    )


def mm(a, b, contract):
    return lax.dot_general(a, b, ((contract[:1], contract[1:]), ((), ())), preferred_element_type=jnp.float32)


def word_pieces(count):
    pieces, start = [], 0
    while start < count:
        size = 16 if count - start >= 16 else 8
        pieces.append((start, size))
        start += size
    return pieces


def kept_places(words):
    rest = words.astype(jnp.float32)
    digits = []
    for _ in range(3):
        above = jnp.floor((rest + 0.5) * (1.0 / 6.0))
        digits.append(rest - 6.0 * above)
        rest = above
    digits.append(rest)
    pattern = jnp.concatenate(digits, axis=0)
    three = jnp.where(pattern >= 3.0, 1.0, 0.0)
    five = jnp.where(pattern >= 5.0, 1.0, 0.0)
    return three + five, pattern + 1.0 - 2.0 * three - five


def value_order(size):
    n = 8 * size
    row = lax.broadcasted_iota(jnp.int32, (n, n), 0)
    col = lax.broadcasted_iota(jnp.int32, (n, n), 1)
    want = (col % 2) * (4 * size) + (col // 2 % 4) * size + col // 8
    return jnp.where(row == want, 1.0, 0.0).astype(jnp.bfloat16)


def dense_order(size):
    n = 16 * size
    row = lax.broadcasted_iota(jnp.int32, (n, n), 0)
    col = lax.broadcasted_iota(jnp.int32, (n, n), 1)
    want = (col % 4) * (4 * size) + (col // 4 % 4) * size + col // 16
    return jnp.where(row == want, 1.0, 0.0).astype(jnp.bfloat16)


def expand_body(values_ref, words_ref, dense_ref):
    for start, size in word_pieces(words_ref.shape[0]):
        lead, trail = kept_places(words_ref[start : start + size, :])
        both = mm(value_order(size), values_ref[8 * start : 8 * (start + size), :], (1, 0))
        half = 4 * size
        lead_vals, trail_vals = both[:half], both[half:]
        placed = jnp.concatenate(
            [
                jnp.where(lead == p, lead_vals, jnp.where(trail == p, trail_vals, 0.0))
                for p in (0.0, 1.0, 2.0, 3.0)
            ],
            axis=0,
        ).astype(jnp.bfloat16)
        dense_ref[16 * start : 16 * (start + size), :] = mm(dense_order(size), placed, (0, 0)).astype(
            jnp.bfloat16
        )


def expand(values, words, row_blocks, col_blocks):
    rows, cols = words.shape[0] // row_blocks, words.shape[1] // col_blocks
    at = lambda i: (i if row_blocks > 1 else 0, i if col_blocks > 1 else 0)
    return call(
        expand_body,
        grid=(row_blocks * col_blocks,),
        in_specs=[pl.BlockSpec((8 * rows, cols), at), pl.BlockSpec((rows, cols), at)],
        out_specs=pl.BlockSpec((16 * rows, cols), at),
        out_shape=jax.ShapeDtypeStruct((16 * words.shape[0], words.shape[1]), jnp.bfloat16),
        cost_estimate=pl.CostEstimate(flops=10**9 * 4, bytes_accessed=3 * 10**7, transcendentals=0),
    )(values, words)


def compress_into(dense, words_ref, out_ref):
    for start, size in word_pieces(words_ref.shape[0]):
        lead, trail = kept_places(words_ref[start : start + size, :])
        ordered = mm(dense_order(size), dense[16 * start : 16 * (start + size)], (1, 0))
        half = 4 * size
        lead_vals = jnp.zeros(lead.shape, jnp.float32)
        trail_vals = lead_vals
        for p in range(4):
            part = ordered[p * half : (p + 1) * half]
            lead_vals = jnp.where(lead == float(p), part, lead_vals)
            trail_vals = jnp.where(trail == float(p), part, trail_vals)
        both = jnp.concatenate([lead_vals, trail_vals], axis=0).astype(jnp.bfloat16)
        out_ref[8 * start : 8 * (start + size), :] = mm(value_order(size), both, (0, 0)).astype(
            jnp.bfloat16
        )


def swiglu_body(last, hidden_first, row_ref, cot_ref, gate_ref, up_ref, down_ref, *rest):
    hidden_ref, gate_grad_ref, up_grad_ref, gate_acc, up_acc, hid_acc = rest
    step = pl.program_id(0)

    @pl.when(step == 0)
    def _():
        gate_acc[...] = jnp.zeros_like(gate_acc)
        up_acc[...] = jnp.zeros_like(up_acc)
        hid_acc[...] = jnp.zeros_like(hid_acc)

    gate_acc[...] += mm(row_ref[0], gate_ref[...], (1, 0))
    up_acc[...] += mm(row_ref[0], up_ref[...], (1, 0))
    hid_acc[...] += mm(cot_ref[0], down_ref[...], (1, 1 if hidden_first else 0))

    @pl.when(step == last)
    def _():
        gate_pre, up_pre, hid_grad = gate_acc[...], up_acc[...], hid_acc[...]
        sig = jax.nn.sigmoid(gate_pre)
        active = gate_pre * sig
        hidden_ref[...] = (active * up_pre).astype(jnp.bfloat16)
        gate_grad_ref[...] = (hid_grad * up_pre * sig * (1.0 + gate_pre * (1.0 - sig))).astype(
            jnp.bfloat16
        )
        up_grad_ref[...] = (hid_grad * active).astype(jnp.bfloat16)


def swiglu_steps(both, w_gate, w_up, w_down, hidden_first):
    parts, rows, width = both.shape
    width //= 2
    hid = w_gate.shape[1]
    weight = pl.BlockSpec((width, hid), lambda i: (i, 0))
    down = pl.BlockSpec((hid, width), lambda i: (0, i)) if hidden_first else weight
    return call(
        functools.partial(swiglu_body, parts - 1, hidden_first),
        grid=(parts,),
        in_specs=[
            pl.BlockSpec((1, rows, width), lambda i: (i, 0, 0)),
            pl.BlockSpec((1, rows, width), lambda i: (i, 0, 1)),
            weight,
            weight,
            down,
        ],
        out_specs=[pl.BlockSpec((rows, hid), lambda i: (0, 0))] * 3,
        out_shape=[jax.ShapeDtypeStruct((rows, hid), jnp.bfloat16)] * 3,
        scratch_shapes=[pltpu.VMEM((rows, hid), jnp.float32)] * 3,
        cost_estimate=pl.CostEstimate(
            flops=6 * rows * hid * width * parts, bytes_accessed=2 * 10**7, transcendentals=rows * hid
        ),
    )(both, both, w_gate, w_up, w_down)


def back_body(gate_grad_ref, up_grad_ref, gate_ref, up_ref, out_ref):
    out_ref[0] = (
        mm(gate_grad_ref[...], gate_ref[...], (1, 1)) + mm(up_grad_ref[...], up_ref[...], (1, 1))
    ).astype(out_ref.dtype)


def back(gate_grad, up_grad, w_gate, w_up, parts):
    rows, hid = gate_grad.shape
    width = w_gate.shape[0] // parts
    whole = pl.BlockSpec((rows, hid), lambda i: (0, 0))
    weight = pl.BlockSpec((width, hid), lambda i: (i, 0))
    return call(
        back_body,
        grid=(parts,),
        in_specs=[whole, whole, weight, weight],
        out_specs=pl.BlockSpec((1, rows, width), lambda i: (i, 0, 0)),
        out_shape=jax.ShapeDtypeStruct((parts, rows, width), jnp.bfloat16),
        cost_estimate=pl.CostEstimate(
            flops=4 * rows * hid * width * parts, bytes_accessed=2 * 10**7, transcendentals=0
        ),
    )(gate_grad, up_grad, w_gate, w_up)


def gate_up_body(row_ref, gate_grad_ref, up_grad_ref, gate_words, up_words, gate_out, up_out):
    rows = row_ref[0]
    compress_into(mm(rows, gate_grad_ref[...], (0, 0)).astype(jnp.bfloat16), gate_words, gate_out)
    compress_into(mm(rows, up_grad_ref[...], (0, 0)).astype(jnp.bfloat16), up_words, up_out)


def gate_up_values(both, gate_grad, up_grad, gate_words, up_words):
    parts, rows, width = both.shape
    width //= 2
    hid = gate_grad.shape[1]
    grads = pl.BlockSpec((rows, hid), lambda i: (0, 0))
    words = pl.BlockSpec((width // 16, hid), lambda i: (i, 0))
    return call(
        gate_up_body,
        grid=(parts,),
        in_specs=[pl.BlockSpec((1, rows, width), lambda i: (i, 0, 0)), grads, grads, words, words],
        out_specs=[pl.BlockSpec((width // 2, hid), lambda i: (i, 0))] * 2,
        out_shape=[jax.ShapeDtypeStruct((parts * width // 2, hid), jnp.bfloat16)] * 2,
        cost_estimate=pl.CostEstimate(
            flops=8 * rows * hid * width * parts, bytes_accessed=2 * 10**7, transcendentals=0
        ),
    )(both, gate_grad, up_grad, gate_words, up_words)


def down_body(hidden_ref, cot_ref, words_ref, out_ref):
    compress_into(mm(hidden_ref[...], cot_ref[0], (0, 0)).astype(jnp.bfloat16), words_ref, out_ref)


def down_values_of(both, hidden, words):
    parts, rows, width = both.shape
    width //= 2
    hid = hidden.shape[1]
    return call(
        down_body,
        grid=(parts,),
        in_specs=[
            pl.BlockSpec((rows, hid), lambda i: (0, 0)),
            pl.BlockSpec((1, rows, width), lambda i: (i, 0, 1)),
            pl.BlockSpec((hid // 16, width), lambda i: (0, i)),
        ],
        out_specs=pl.BlockSpec((hid // 2, width), lambda i: (0, i)),
        out_shape=jax.ShapeDtypeStruct((hid // 2, parts * width), jnp.bfloat16),
        cost_estimate=pl.CostEstimate(
            flops=4 * rows * hid * width * parts, bytes_accessed=2 * 10**7, transcendentals=0
        ),
    )(hidden, both, words)


def weight_body(row_ref, cot_ref, gate_grad_ref, up_grad_ref, hidden_ref, *outs):
    rows, cots = row_ref[0], cot_ref[0]
    outs[0][...] = mm(rows, gate_grad_ref[...], (0, 0)).astype(jnp.bfloat16)
    outs[1][...] = mm(rows, up_grad_ref[...], (0, 0)).astype(jnp.bfloat16)
    outs[2][...] = mm(cots, hidden_ref[...], (0, 0)).astype(jnp.bfloat16)


def weight_grads(both, gate_grad, up_grad, hidden):
    parts, rows, width = both.shape
    width //= 2
    hid = hidden.shape[1]
    steps = pl.BlockSpec((rows, hid), lambda i: (0, 0))
    return call(
        weight_body,
        grid=(parts,),
        in_specs=[
            pl.BlockSpec((1, rows, width), lambda i: (i, 0, 0)),
            pl.BlockSpec((1, rows, width), lambda i: (i, 0, 1)),
            steps,
            steps,
            steps,
        ],
        out_specs=[pl.BlockSpec((width, hid), lambda i: (i, 0))] * 3,
        out_shape=[jax.ShapeDtypeStruct((parts * width, hid), jnp.bfloat16)] * 3,
        cost_estimate=pl.CostEstimate(
            flops=6 * rows * hid * width * parts, bytes_accessed=2 * 10**7, transcendentals=0
        ),
    )(both, both, gate_grad, up_grad, hidden)


def slot_masks(route_block, weight_block, experts, capacity):
    flat = route_block.reshape(-1)
    count = flat.shape[0]
    place = jnp.arange(count, dtype=jnp.int32)
    same = (flat[:, None] == flat[None, :]) & (place[None, :] < place[:, None])
    slot_index = flat * capacity + jnp.sum(same, axis=1, dtype=jnp.int32)
    slots = jnp.arange(experts * capacity, dtype=jnp.int32)
    first, second = slot_index.reshape(-1, 2)[:, 0], slot_index.reshape(-1, 2)[:, 1]
    hit_first = slots[:, None] == first[None, :]
    hit_second = slots[:, None] == second[None, :]
    taken = (hit_first | hit_second).astype(jnp.bfloat16)
    scales = jnp.sum(
        jnp.where(hit_first, weight_block[None, :, 0], 0.0)
        + jnp.where(hit_second, weight_block[None, :, 1], 0.0),
        axis=1,
    )
    return taken, scales


def shards(
    tokens,
    cotangent,
    routes,
    route_weights,
    gate_values,
    up_values,
    down_values,
    gate_words,
    up_words,
    down_words,
    res_gate,
    res_up,
    res_down,
):
    experts = lax.axis_size("expert")
    dp_count = lax.axis_size("dp")
    parts = lax.axis_size("tensor")
    tok_count, width = tokens.shape
    capacity = 5 * tok_count // (2 * experts)
    local = jnp.concatenate([tokens, cotangent], axis=1)
    pair_local = lax.all_gather(local, "dp", axis=0, tiled=True)
    pair_both = lax.all_gather(pair_local, "tensor", axis=0)
    taken, scales = slot_masks(routes, route_weights, experts, capacity)
    slot_local = mm(taken, local, (1, 0))
    slot_local = jnp.concatenate(
        [slot_local[:, :width], slot_local[:, width:] * scales[:, None]], axis=1
    ).astype(jnp.bfloat16)
    slot_local = lax.all_to_all(
        slot_local.reshape(experts, capacity, 2 * width), "expert", split_axis=0, concat_axis=0, tiled=True
    ).reshape(experts * capacity, 2 * width)
    slot_both = lax.all_gather(slot_local, "tensor", axis=0)

    gate_dense = expand(gate_values[0], gate_words[0], parts, 1)
    up_dense = expand(up_values[0], up_words[0], parts, 1)
    down_dense = expand(down_values[0], down_words[0], 1, parts)

    res_hidden, res_gate_step, res_up_step = swiglu_steps(pair_both, res_gate, res_up, res_down, False)
    res_back = back(res_gate_step, res_up_step, res_gate, res_up, parts)
    res_terms = weight_grads(pair_both, res_gate_step, res_up_step, res_hidden)

    hidden, gate_grad, up_grad = swiglu_steps(slot_both, gate_dense, up_dense, down_dense, True)
    slot_back = back(gate_grad, up_grad, gate_dense, up_dense, parts)
    gate_terms, up_terms = gate_up_values(slot_both, gate_grad, up_grad, gate_words[0], up_words[0])
    down_terms = down_values_of(slot_both, hidden, down_words[0])

    both_back = jnp.concatenate([slot_back, res_back], axis=1)
    both_share = lax.psum_scatter(both_back, "tensor", scatter_dimension=0, tiled=True)[0]
    slot_count = experts * capacity
    returned = lax.all_to_all(
        both_share[:slot_count].reshape(experts, capacity, width),
        "expert",
        split_axis=0,
        concat_axis=0,
        tiled=True,
    ).reshape(slot_count, width)
    res_share = lax.psum_scatter(both_share[slot_count:], "dp", scatter_dimension=0, tiled=True)
    combined = res_share.astype(jnp.float32) + mm(taken, returned, (0, 0))

    gate_share = lax.psum_scatter(gate_terms, "dp", scatter_dimension=0, tiled=True)
    up_share = lax.psum_scatter(up_terms, "dp", scatter_dimension=0, tiled=True)
    down_share = lax.psum_scatter(down_terms, "dp", scatter_dimension=1, tiled=True)
    res_sums = [lax.psum_scatter(term, "expert", scatter_dimension=0, tiled=True) for term in res_terms]
    return (
        combined.astype(jnp.bfloat16),
        gate_share[None],
        up_share[None],
        down_share[None],
        res_sums[0],
        res_sums[1],
        res_sums[2],
    )


def solution(mesh):
    in_specs = (
        P(("dp", "expert"), "tensor"),
        P(("dp", "expert"), "tensor"),
        P(("dp", "expert"), None),
        P(("dp", "expert"), None),
        P("expert", None, "tensor"),
        P("expert", None, "tensor"),
        P("expert", "tensor", None),
        P("expert", None, "tensor"),
        P("expert", None, "tensor"),
        P("expert", "tensor", None),
        P(None, ("dp", "tensor")),
        P(None, ("dp", "tensor")),
        P(None, ("dp", "tensor")),
    )
    out_specs = (
        P(("dp", "expert"), "tensor"),
        P("expert", "dp", "tensor"),
        P("expert", "dp", "tensor"),
        P("expert", "tensor", "dp"),
        P("expert", ("dp", "tensor")),
        P("expert", ("dp", "tensor")),
        P("expert", ("dp", "tensor")),
    )
    return jax.shard_map(shards, mesh=mesh, in_specs=in_specs, out_specs=out_specs, check_vma=False)
```

time: 804 us -> 478 us (0.59); the launches traced: 794 us -> 477 us
  local copies, waits for them, and re-layouts: 359 us -> 5.35 us
  Pallas kernels: 0 us -> 89.3 us
  matrix products: 87.6 us -> 2.44 us
  blocking collectives: 22.8 us -> 82.6 us
  other arithmetic: 25.1 us -> 4.53 us
  starting transfers between devices: 16.3 us -> 0.58 us
  waiting for transfers between devices: 267 us -> 278 us
    reduce_scatter x5 -> x8, waiting for transfers between devices: 110 us -> 275 us  [the longest x3 121 us: shards(): lax.psum_scatter(term, 'expert', scatter_dimension=0, tiled=True)]
    unnamed x13 -> x10, waiting for transfers between devices: 103 us -> 2.02 us
    pallas_call x0 -> x10, Pallas kernels: none -> 89.3 us  [the longest x3 22.9 us: expand(): call(expand_body, grid=(row_blocks * col_blocks,), in_specs=[pl.BlockSpec...]
    dot_general x16 -> x2, matrix products: 87.6 us -> 2.44 us  [mm(): lax.dot_general(a, b, ((contract[:1], contract[1:]), ((), ())), preferred...]
    eq x12 -> x2, local copies, waits for them, and re-layouts: 73.4 us -> 0.15 us  [the longest x1 0.14 us: slot_masks(): same = (flat[:, None] == flat[None, :]) & (place[None, :] < place[:, None])]
    all_to_all x0 -> x2, blocking collectives: none -> 68.3 us  [the longest x1 36.3 us: shards(): lax.all_to_all(both_share[:slot_count].reshape(experts, capacity, width),...]
    broadcast_in_dim x11 -> x1, local copies, waits for them, and re-layouts: 55.7 us -> 0.01 us  [slot_masks(): jnp.where(hit_first, weight_block[None, :, 0], 0.0)]
    all_to_all x3 -> x0, waiting for transfers between devices: 54.4 us -> none  [the longest x1 54.4 us: shards(): lax.all_to_all(shares, 'expert', split_axis=0, concat_axis=0, tiled=True)]
  transfers between devices with their start and end apart: 13 -> 10, of which waited for: 6 -> 8; matrix products, arithmetic and copies ran while one was open for 58% -> 1% of each run, Pallas kernels for 0% -> 15%
where the time goes in v1:
time: 478 us; the launch traced here: 477 us
  waiting for transfers between devices  278 us (58%)
  Pallas kernels  89.3 us (19%)
  blocking collectives  82.6 us (17%)
  between operations  14.3 us (3%)
  local copies, waits for them, and re-layouts  5.35 us (1%)
    reduce_scatter x3, waiting for transfers between devices, shards(): lax.psum_scatter(term, 'expert', scatter_dimension=0, tiled=True)  121 us
    reduce_scatter x1, waiting for transfers between devices, shards(): lax.psum_scatter(both_back, 'tensor', scatter_dimension=0, tiled=True)[0]  44.2 us
    reduce_scatter x1, waiting for transfers between devices, shards(): up_share = lax.psum_scatter(up_terms, 'dp', scatter_dimension=0, tiled=True)  36.9 us
    reduce_scatter x1, waiting for transfers between devices, shards(): lax.psum_scatter(down_terms, 'dp', scatter_dimension=1, tiled=True)  36.7 us
    reduce_scatter x1, waiting for transfers between devices, shards(): lax.psum_scatter(gate_terms, 'dp', scatter_dimension=0, tiled=True)  36.6 us
    all_to_all x1, blocking collectives, shards(): lax.all_to_all(both_share[:slot_count].reshape(experts, capacity, width),...  36.3 us
    all_to_all x1, blocking collectives, shards(): lax.all_to_all(slot_local.reshape(experts, capacity, 2 * width), 'expert'...  32 us
    pallas_call x3, Pallas kernels, expand(): call(expand_body, grid=(row_blocks * col_blocks,), in_specs=[pl.BlockSpec...  22.9 us
  transfers between devices with their start and end apart: 10, of which 8 were waited for; matrix products, arithmetic and copies ran while one was open for 1% of the time, Pallas kernels for 15%

profile of v1, /device:TPU:0, one launch (start us, length us, event | category | flops | bytes accessed | tf_op | source)
XLA Modules:
  0.0 477.5 jit_solution(5014240494230612828)
XLA Ops:
  7.2 1.0 constant_dynamic-update-slice_fusion.1
  8.2 1.0 constant_dynamic-update-slice_fusion
  9.2 14.2 %all_gather.13 = bf16[256,1792]{1,0:T(8,128)(2,1)} all-gather(bf16[128,1792]{1,0:T(8,128)(2,1)S(1)} %constant_dynamic-update-slice_fusion), channel_id=1, replica_groups=mesh['dp'=2,'expert'=4,'tensor'=4] {'dp'}, dimensions={0}, use_global_device_ids=true | all-gather | bytes 1376256 | tf_op jit(solution)/shard_map/all_gather | solution.py:304
  24.1 0.5 fusion.5
  25.1 32.0 %all_to_all.10 = bf16[4,80,1792]{2,1,0:T(8,128)(2,1)} all-to-all(bf16[4,80,1792]{2,1,0:T(8,128)(2,1)S(1)} %pad_maximum_fusion.1), channel_id=1, replica_groups=mesh['dp'=2,'expert'=4,'tensor'=4] {'expert'}, dimensions={0} | all-to-all | bytes 2293760 | tf_op jit(solution)/shard_map/all_to_all | solution.py:311
  57.2 7.7 %shard_map.180.gate_ref = bf16[3584,640]{1,0:T(8,128)(2,1)} custom-call(bf16[1792,640]{1,0:T(8,128)(2,1)} %bitcast.36, s32[224,640]{1,0:T(8,128)} %bitcast.42), custom_call_target="tpu_custom_call" | custom-call | flops 4000000000 | bytes 30000000 | tf_op jit(solution)/shard_map/pallas_call | solution.py:85
  64.9 7.7 %shard_map.181.up_ref = bf16[3584,640]{1,0:T(8,128)(2,1)} custom-call(bf16[1792,640]{1,0:T(8,128)(2,1)} %bitcast.37, s32[224,640]{1,0:T(8,128)} %bitcast.44), custom_call_target="tpu_custom_call" | custom-call | flops 4000000000 | bytes 30000000 | tf_op jit(solution)/shard_map/pallas_call | solution.py:85
  72.6 7.5 %shard_map.182.down_ref = bf16[640,3584]{1,0:T(8,128)(2,1)} custom-call(bf16[320,3584]{1,0:T(8,128)(2,1)} %bitcast.38, s32[40,3584]{1,0:T(8,128)} %bitcast.46), custom_call_target="tpu_custom_call" | custom-call | flops 4000000000 | bytes 30000000 | tf_op jit(solution)/shard_map/pallas_call | solution.py:85
  80.1 7.8 %shard_map.185 = (bf16[256,384]{1,0:T(8,128)(2,1)}, bf16[256,384]{1,0:T(8,128)(2,1)}, bf16[256,384]{1,0:T(8,128)(2,1)}) custom-call(bf16[4,256,1792]{2,1,0:T(8,128)(2,1)} %bitcast.27, bf16[4,256,1792]{2,1,0:T(8,128)(2,1)} %bitcast.28, bf16[3584,384]{1,0:T(8,128)(2,1)} %gate_ref.3, bf16[3584,384]{1,0:T(8,128)(2,1)} %up_ref.3, bf16[3584,384]{1,0:T(8,128)(2,1)} %down_ref.1), custom_call_target="tpu_custom_call" | custom-call | flops 2113929216 | bytes 20000000 | tf_op jit(solution)/shard_map/pallas_call | solution.py:144
  87.9 6.1 %shard_map.186 = bf16[4,256,896]{2,1,0:T(8,128)(2,1)} custom-call(bf16[256,384]{1,0:T(8,128)(2,1)} %get-tuple-element.20.gate_grad_ref, bf16[256,384]{1,0:T(8,128)(2,1)} %get-tuple-element.21.up_grad_ref, bf16[3584,384]{1,0:T(8,128)(2,1)} %gate_ref.3, bf16[3584,384]{1,0:T(8,128)(2,1)} %up_ref.3), custom_call_target="tpu_custom_call" | custom-call | flops 1409286144 | bytes 20000000 | tf_op jit(solution)/shard_map/pallas_call | solution.py:174
  94.0 0.9 all-gather.4.cloned.1.call-done.row_ref.cot_ref
  94.9 11.4 %shard_map.183 = (bf16[320,640]{1,0:T(8,128)(2,1)}, bf16[320,640]{1,0:T(8,128)(2,1)}, bf16[320,640]{1,0:T(8,128)(2,1)}) custom-call(bf16[4,320,1792]{2,1,0:T(8,128)(2,1)} %all-gather.4.cloned.1.call-done.row_ref.cot_ref, bf16[4,320,1792]{2,1,0:T(8,128)(2,1)} %all-gather.4.cloned.1.call-done.row_ref.cot_ref, bf16[3584,640]{1,0:T(8,128)(2,1)} %shard_map.180.gate_ref, ...), custom_call_target="tpu_custom_call" | custom-call | flops 4404019200 | bytes 20000000 | tf_op jit(solution)/shard_map/pallas_call | solution.py:144
  106.3 8.4 %shard_map.184 = bf16[4,320,896]{2,1,0:T(8,128)(2,1)} custom-call(bf16[320,640]{1,0:T(8,128)(2,1)} %get-tuple-element.18.gate_grad_ref, bf16[320,640]{1,0:T(8,128)(2,1)} %get-tuple-element.19.up_grad_ref, bf16[3584,640]{1,0:T(8,128)(2,1)} %shard_map.180.gate_ref, bf16[3584,640]{1,0:T(8,128)(2,1)} %shard_map.181.up_ref), custom_call_target="tpu_custom_call" | custom-call | flops 2936012800 | bytes 20000000 | tf_op jit(solution)/shard_map/pallas_call | solution.py:174
  114.7 4.0 pad_maximum_fusion
  118.8 44.2 %reduce-scatter.9.cloned.1.call-done = bf16[1,576,896]{2,1,0:T(8,128)(2,1)} async-done(((bf16[4,576,896]{2,1,0:T(8,128)(2,1)}), bf16[1,576,896]{2,1,0:T(8,128)(2,1)}) %reduce-scatter.9.cloned.1.call-update) | async-done | bytes 1032208 | tf_op jit(solution)/shard_map/reduce_scatter | solution.py:330
  163.0 1.9 slice_bitcast_fusion
  164.9 6.6 %shard_map.189 = (bf16[3584,384]{1,0:T(8,128)(2,1)}, bf16[3584,384]{1,0:T(8,128)(2,1)}, bf16[3584,384]{1,0:T(8,128)(2,1)}) custom-call(bf16[4,256,1792]{2,1,0:T(8,128)(2,1)} %bitcast.29, bf16[4,256,1792]{2,1,0:T(8,128)(2,1)} %bitcast.30, bf16[256,384]{1,0:T(8,128)(2,1)} %get-tuple-element.20.gate_grad_ref, bf16[256,384]{1,0:T(8,128)(2,1)} %get-tuple-element.21.up_grad_ref, ...), custom_call_target="tpu_custom_call" | custom-call | flops 2113929216 | bytes 20000000 | tf_op jit(solution)/shard_map/pallas_call | solution.py:246
  171.5 0.5 reduce-scatter.21.cloned.1.call-update
  172.1 0.7 reduce-scatter.23.cloned.1.call-update
  172.8 0.2 reduce-scatter.13.cloned.1.call-start
  173.0 16.9 %shard_map.187 = (bf16[1792,640]{1,0:T(8,128)(2,1)}, bf16[1792,640]{1,0:T(8,128)(2,1)}) custom-call(bf16[4,320,1792]{2,1,0:T(8,128)(2,1)} %all-gather.4.cloned.1.call-done.row_ref.cot_ref, bf16[320,640]{1,0:T(8,128)(2,1)} %get-tuple-element.18.gate_grad_ref, bf16[320,640]{1,0:T(8,128)(2,1)} %get-tuple-element.19.up_grad_ref, s32[224,640]{1,0:T(8,128)} %bitcast.43, ...), custom_call_target="tpu_custom_call" | custom-call | flops 5872025600 | bytes 20000000 | tf_op jit(solution)/shard_map/pallas_call | solution.py:198
  190.0 0.7 reduce-scatter.15.cloned.1.call-update
  190.8 9.2 %shard_map.188 = bf16[320,3584]{1,0:T(8,128)(2,1)} custom-call(bf16[320,640]{1,0:T(8,128)(2,1)} %get-tuple-element.24.hidden_ref, bf16[4,320,1792]{2,1,0:T(8,128)(2,1)} %all-gather.4.cloned.1.call-done.row_ref.cot_ref, s32[40,3584]{1,0:T(8,128)} %bitcast.47), custom_call_target="tpu_custom_call" | custom-call | flops 2936012800 | bytes 20000000 | tf_op jit(solution)/shard_map/pallas_call | solution.py:218
  200.0 1.0 slice-done
  201.0 36.3 %all_to_all.11 = bf16[4,80,896]{2,1,0:T(8,128)(2,1)S(1)} all-to-all(bf16[4,80,896]{2,1,0:T(8,128)(2,1)S(1)} %bitcast.35), channel_id=1, replica_groups=mesh['dp'=2,'expert'=4,'tensor'=4] {'expert'}, dimensions={0} | all-to-all | bytes 1146880 | tf_op jit(solution)/shard_map/all_to_all | solution.py:332
  237.4 2.0 fusion
  239.4 5.7 %reduce-scatter.19.cloned.1.call-done = bf16[896,384]{1,0:T(8,128)(2,1)} async-done(((bf16[3584,384]{1,0:T(8,128)(2,1)}), bf16[896,384]{1,0:T(8,128)(2,1)}) %reduce-scatter.19.cloned.1.call-update) | async-done | bytes 688144 | tf_op jit(solution)/shard_map/reduce_scatter | solution.py:345
  245.1 58.4 %reduce-scatter.21.cloned.1.call-done = bf16[896,384]{1,0:T(8,128)(2,1)} async-done(((bf16[3584,384]{1,0:T(8,128)(2,1)}), bf16[896,384]{1,0:T(8,128)(2,1)}) %reduce-scatter.21.cloned.1.call-update) | async-done | bytes 688144 | tf_op jit(solution)/shard_map/reduce_scatter | solution.py:345
  303.5 56.8 %reduce-scatter.23.cloned.1.call-done = bf16[896,384]{1,0:T(8,128)(2,1)} async-done(((bf16[3584,384]{1,0:T(8,128)(2,1)}), bf16[896,384]{1,0:T(8,128)(2,1)}) %reduce-scatter.23.cloned.1.call-update) | async-done | bytes 688144 | tf_op jit(solution)/shard_map/reduce_scatter | solution.py:345
  360.3 36.6 %reduce-scatter.13.cloned.1.call-done = bf16[896,640]{1,0:T(8,128)(2,1)} async-done(((bf16[1792,640]{1,0:T(8,128)(2,1)}), bf16[896,640]{1,0:T(8,128)(2,1)}) %reduce-scatter.13.cloned.1.call-update) | async-done | bytes 1146896 | tf_op jit(solution)/shard_map/reduce_scatter | solution.py:342
  397.0 36.9 %reduce-scatter.15.cloned.1.call-done = bf16[896,640]{1,0:T(8,128)(2,1)} async-done(((bf16[1792,640]{1,0:T(8,128)(2,1)}), bf16[896,640]{1,0:T(8,128)(2,1)}) %reduce-scatter.15.cloned.1.call-update) | async-done | bytes 1146896 | tf_op jit(solution)/shard_map/reduce_scatter | solution.py:343
  433.9 36.7 %reduce-scatter.17.cloned.1.call-done = bf16[320,1792]{1,0:T(8,128)(2,1)} async-done(((bf16[320,3584]{1,0:T(8,128)(2,1)}), bf16[320,1792]{1,0:T(8,128)(2,1)}) %reduce-scatter.17.cloned.1.call-update) | async-done | bytes 1146896 | tf_op jit(solution)/shard_map/reduce_scatter | solution.py:344
  (37 shorter events, 1.6 us)
Async XLA Ops:
  7.2 16.3 %copy-start.1 = (s32[128,2]{0,1:T(2,128)S(1)}, s32[128,2]{0,1:T(2,128)}, u32[]{:S(2)}) copy-start(s32[128,2]{0,1:T(2,128)} %param.15) | copy-start | bytes 3076
  7.2 72.9 %all-gather.6.cloned.1.call-start = ((), (), s32[]{:S(2)}) async-start(), calls=%async_computation.19 | async-start | bytes 4587520 | tf_op jit(solution)/shard_map/all_gather | solution.py:305
  23.4 1.3 copy-start.2
  23.4 71.5 %all-gather.4.cloned.1.call-start = ((), (), s32[]{:S(2)}) async-start(), calls=%async_computation.10 | async-start | bytes 5734400 | tf_op jit(solution)/shard_map/all_gather | solution.py:314
  57.1 105.9 %reduce-scatter.9.cloned.1.call-start = ((), (), s32[]{:S(2)}) async-start(), calls=%async_computation.11 | async-start | bytes 5160960 | tf_op jit(solution)/shard_map/reduce_scatter | solution.py:330
  106.3 8.4 %copy-start = (bf16[4,256,896]{2,1,0:T(8,128)(2,1)S(1)}, bf16[4,256,896]{2,1,0:T(8,128)(2,1)}, u32[]{:S(2)}) copy-start(bf16[4,256,896]{2,1,0:T(8,128)(2,1)} %shard_map.186) | copy-start | bytes 5505028
  118.7 118.7 %reduce-scatter.11.cloned.1.call-start = ((), (), s32[]{:S(2)}) async-start(), calls=%async_computation.12 | async-start | bytes 688128 | tf_op jit(solution)/shard_map/reduce_scatter | solution.py:339
  164.8 80.2 %reduce-scatter.19.cloned.1.call-start = ((), (), s32[]{:S(2)}) async-start(), calls=%async_computation.16 | async-start | bytes 3440640 | tf_op jit(solution)/shard_map/reduce_scatter | solution.py:345
  171.5 132.0 %reduce-scatter.21.cloned.1.call-start = ((), (), s32[]{:S(2)}) async-start(), calls=%async_computation.17 | async-start | bytes 3440640 | tf_op jit(solution)/shard_map/reduce_scatter | solution.py:345
  172.1 188.3 %reduce-scatter.23.cloned.1.call-start = ((), (), s32[]{:S(2)}) async-start(), calls=%async_computation.18 | async-start | bytes 3440640 | tf_op jit(solution)/shard_map/reduce_scatter | solution.py:345
  172.8 224.2 %reduce-scatter.13.cloned.1.call-start = ((), (), s32[]{:S(2)}) async-start(), calls=%async_computation.13 | async-start | bytes 3440640 | tf_op jit(solution)/shard_map/reduce_scatter | solution.py:342
  190.0 243.9 %reduce-scatter.15.cloned.1.call-start = ((), (), s32[]{:S(2)}) async-start(), calls=%async_computation.14 | async-start | bytes 3440640 | tf_op jit(solution)/shard_map/reduce_scatter | solution.py:343
  190.7 279.9 %reduce-scatter.17.cloned.1.call-start = ((), (), s32[]{:S(2)}) async-start(), calls=%async_computation.15 | async-start | bytes 3440640 | tf_op jit(solution)/shard_map/reduce_scatter | solution.py:344
  200.0 1.1 slice-start
Sparse Core Ops, SparseCore 0:
  23.5 33.0 all-gather.5
  58.1 36.7 all-gather.3
  118.8 44.0 reduce-scatter.8
  165.2 13.8 reduce-scatter.10
  181.8 63.2 reduce-scatter.18
  247.8 55.6 reduce-scatter.20
  306.4 53.9 reduce-scatter.22
  363.2 33.7 reduce-scatter.12
  399.9 33.9 reduce-scatter.14
  436.6 33.9 reduce-scatter.16

commit v2 on v1

--- a/solution.py
+++ b/solution.py
@@ -231,38 +231,38 @@
     )(hidden, both, words)
 
 
-def weight_body(row_ref, cot_ref, gate_grad_ref, up_grad_ref, hidden_ref, *outs):
+def weight_body(row_ref, cot_ref, steps_ref, *outs):
+    hid = steps_ref.shape[1] // 3
     rows, cots = row_ref[0], cot_ref[0]
-    outs[0][...] = mm(rows, gate_grad_ref[...], (0, 0)).astype(jnp.bfloat16)
-    outs[1][...] = mm(rows, up_grad_ref[...], (0, 0)).astype(jnp.bfloat16)
-    outs[2][...] = mm(cots, hidden_ref[...], (0, 0)).astype(jnp.bfloat16)
-
-
-def weight_grads(both, gate_grad, up_grad, hidden):
+    outs[0][...] = mm(rows, steps_ref[:, :hid], (0, 0)).astype(jnp.bfloat16)
+    outs[1][...] = mm(rows, steps_ref[:, hid : 2 * hid], (0, 0)).astype(jnp.bfloat16)
+    outs[2][...] = mm(cots, steps_ref[:, 2 * hid :], (0, 0)).astype(jnp.bfloat16)
+
+
+def weight_grads(both, steps):
     parts, rows, width = both.shape
     width //= 2
-    hid = hidden.shape[1]
-    steps = pl.BlockSpec((rows, hid), lambda i: (0, 0))
+    hid = steps.shape[1] // 3
+    cuts = 7 if width % 896 == 0 and parts == 1 else 1
+    piece = width // cuts
     return call(
         weight_body,
-        grid=(parts,),
+        grid=(parts, cuts),
         in_specs=[
-            pl.BlockSpec((1, rows, width), lambda i: (i, 0, 0)),
-            pl.BlockSpec((1, rows, width), lambda i: (i, 0, 1)),
-            steps,
-            steps,
-            steps,
+            pl.BlockSpec((1, rows, piece), lambda i, j: (i, 0, j)),
+            pl.BlockSpec((1, rows, piece), lambda i, j: (i, 0, cuts + j)),
+            pl.BlockSpec((rows, 3 * hid), lambda i, j: (0, 0)),
         ],
-        out_specs=[pl.BlockSpec((width, hid), lambda i: (i, 0))] * 3,
+        out_specs=[pl.BlockSpec((piece, hid), lambda i, j: (i * cuts + j, 0))] * 3,
         out_shape=[jax.ShapeDtypeStruct((parts * width, hid), jnp.bfloat16)] * 3,
         cost_estimate=pl.CostEstimate(
             flops=6 * rows * hid * width * parts, bytes_accessed=2 * 10**7, transcendentals=0
         ),
-    )(both, both, gate_grad, up_grad, hidden)
-
-
-def slot_masks(route_block, weight_block, experts, capacity):
-    flat = route_block.reshape(-1)
+    )(both, both, steps)
+
+
+def slot_masks(route_block, weight_block, own, experts, capacity):
+    flat = (route_block.reshape(-1) - own + experts) % experts
     count = flat.shape[0]
     place = jnp.arange(count, dtype=jnp.int32)
     same = (flat[:, None] == flat[None, :]) & (place[None, :] < place[:, None])
@@ -278,6 +278,56 @@
         axis=1,
     )
     return taken, scales
+
+
+def swapped(block, axis, distance):
+    count = lax.axis_size(axis)
+    return lax.ppermute(block, axis, [(i, i ^ distance) for i in range(count)])
+
+
+def shifted(block, axis, distance):
+    count = lax.axis_size(axis)
+    return lax.ppermute(block, axis, [(i, (i + distance) % count) for i in range(count)])
+
+
+def gather_parts(block):
+    if lax.axis_size("tensor") != 4:
+        return lax.all_gather(block, "tensor", axis=0)
+    place = lax.axis_index("tensor")
+    low_chip, low_core = place // 2 == 0, place % 2 == 0
+    far = swapped(block, "tensor", 2)
+    mine = jnp.stack([jnp.where(low_chip, block, far), jnp.where(low_chip, far, block)])
+    near = swapped(mine, "tensor", 1)
+    both = jnp.stack([jnp.where(low_core, mine, near), jnp.where(low_core, near, mine)], axis=1)
+    return both.reshape((4,) + block.shape)
+
+
+def added(a, b):
+    return a.astype(jnp.float32) + b.astype(jnp.float32)
+
+
+def scatter_parts(parts):
+    if lax.axis_size("tensor") != 4:
+        return lax.psum_scatter(parts, "tensor", scatter_dimension=0, tiled=True)[0].astype(jnp.float32)
+    place = lax.axis_index("tensor")
+    chip, core = place // 2, place % 2
+    split = parts.reshape((2, 2) + parts.shape[1:])
+    send = lax.dynamic_index_in_dim(split, 1 - core, 1, keepdims=False)
+    keep = lax.dynamic_index_in_dim(split, core, 1, keepdims=False)
+    summed = added(keep, swapped(send, "tensor", 1)).astype(jnp.bfloat16)
+    send = lax.dynamic_index_in_dim(summed, 1 - chip, 0, keepdims=False)
+    keep = lax.dynamic_index_in_dim(summed, chip, 0, keepdims=False)
+    return added(keep, swapped(send, "tensor", 2))
+
+
+def scatter_batches(block, axis):
+    if lax.axis_size("dp") != 2:
+        return lax.psum_scatter(block, "dp", scatter_dimension=axis, tiled=True).astype(jnp.float32)
+    own = lax.axis_index("dp")
+    size = block.shape[axis] // 2
+    send = lax.dynamic_slice_in_dim(block, (1 - own) * size, size, axis)
+    keep = lax.dynamic_slice_in_dim(block, own * size, size, axis)
+    return added(keep, swapped(send, "dp", 1))
 
 
 def shards(
@@ -301,17 +351,18 @@
     tok_count, width = tokens.shape
     capacity = 5 * tok_count // (2 * experts)
     local = jnp.concatenate([tokens, cotangent], axis=1)
-    pair_local = lax.all_gather(local, "dp", axis=0, tiled=True)
-    pair_both = lax.all_gather(pair_local, "tensor", axis=0)
-    taken, scales = slot_masks(routes, route_weights, experts, capacity)
+    taken, scales = slot_masks(routes, route_weights, lax.axis_index("expert"), experts, capacity)
     slot_local = mm(taken, local, (1, 0))
     slot_local = jnp.concatenate(
         [slot_local[:, :width], slot_local[:, width:] * scales[:, None]], axis=1
     ).astype(jnp.bfloat16)
-    slot_local = lax.all_to_all(
-        slot_local.reshape(experts, capacity, 2 * width), "expert", split_axis=0, concat_axis=0, tiled=True
-    ).reshape(experts * capacity, 2 * width)
-    slot_both = lax.all_gather(slot_local, "tensor", axis=0)
+    blocks = [slot_local[k * capacity : (k + 1) * capacity] for k in range(experts)]
+    arrived = [blocks[0]] + [shifted(blocks[k], "expert", k) for k in range(1, experts)]
+    slot_both = gather_parts(jnp.concatenate(arrived, axis=0))
+
+    pair_both = lax.all_gather(local, ("tensor", "dp"), axis=0).reshape(
+        parts, dp_count * tok_count, 2 * width
+    )
 
     gate_dense = expand(gate_values[0], gate_words[0], parts, 1)
     up_dense = expand(up_values[0], up_words[0], parts, 1)
@@ -319,35 +370,43 @@
 
     res_hidden, res_gate_step, res_up_step = swiglu_steps(pair_both, res_gate, res_up, res_down, False)
     res_back = back(res_gate_step, res_up_step, res_gate, res_up, parts)
-    res_terms = weight_grads(pair_both, res_gate_step, res_up_step, res_hidden)
 
     hidden, gate_grad, up_grad = swiglu_steps(slot_both, gate_dense, up_dense, down_dense, True)
     slot_back = back(gate_grad, up_grad, gate_dense, up_dense, parts)
     gate_terms, up_terms = gate_up_values(slot_both, gate_grad, up_grad, gate_words[0], up_words[0])
     down_terms = down_values_of(slot_both, hidden, down_words[0])
 
-    both_back = jnp.concatenate([slot_back, res_back], axis=1)
-    both_share = lax.psum_scatter(both_back, "tensor", scatter_dimension=0, tiled=True)[0]
-    slot_count = experts * capacity
-    returned = lax.all_to_all(
-        both_share[:slot_count].reshape(experts, capacity, width),
-        "expert",
-        split_axis=0,
-        concat_axis=0,
-        tiled=True,
-    ).reshape(slot_count, width)
-    res_share = lax.psum_scatter(both_share[slot_count:], "dp", scatter_dimension=0, tiled=True)
-    combined = res_share.astype(jnp.float32) + mm(taken, returned, (0, 0))
-
-    gate_share = lax.psum_scatter(gate_terms, "dp", scatter_dimension=0, tiled=True)
-    up_share = lax.psum_scatter(up_terms, "dp", scatter_dimension=0, tiled=True)
-    down_share = lax.psum_scatter(down_terms, "dp", scatter_dimension=1, tiled=True)
-    res_sums = [lax.psum_scatter(term, "expert", scatter_dimension=0, tiled=True) for term in res_terms]
+    slot_share = scatter_parts(slot_back).astype(jnp.bfloat16)
+    blocks = [slot_share[k * capacity : (k + 1) * capacity] for k in range(experts)]
+    returned = [blocks[0]] + [shifted(blocks[k], "expert", -k) for k in range(1, experts)]
+    res_share = scatter_batches(scatter_parts(res_back).astype(jnp.bfloat16), 0)
+    combined = res_share + mm(taken, jnp.concatenate(returned, axis=0), (0, 0))
+
+    gate_share = scatter_batches(gate_terms, 0)
+    up_share = scatter_batches(up_terms, 0)
+    down_share = scatter_batches(down_terms, 1)
+
+    if parts == experts:
+        turned = lax.ppermute(
+            local,
+            ("expert", "tensor"),
+            [(e * parts + t, t * parts + e) for e in range(experts) for t in range(parts)],
+        )
+        all_rows = lax.all_gather(turned, ("tensor", "dp"), axis=0).reshape(1, -1, 2 * width)
+        steps = jnp.concatenate([res_gate_step, res_up_step, res_hidden], axis=1)
+        steps = lax.all_gather(steps, "expert", axis=0, tiled=True)
+        res_sums = weight_grads(all_rows, steps)
+    else:
+        steps = jnp.concatenate([res_gate_step, res_up_step, res_hidden], axis=1)
+        res_sums = [
+            lax.psum_scatter(term, "expert", scatter_dimension=0, tiled=True)
+            for term in weight_grads(pair_both, steps)
+        ]
     return (
         combined.astype(jnp.bfloat16),
-        gate_share[None],
-        up_share[None],
-        down_share[None],
+        gate_share.astype(jnp.bfloat16)[None],
+        up_share.astype(jnp.bfloat16)[None],
+        down_share.astype(jnp.bfloat16)[None],
         res_sums[0],
         res_sums[1],
         res_sums[2],

time: 478 us -> 249 us (0.52)
  waiting for transfers between devices: 278 us -> 80.6 us
  blocking collectives: 82.6 us -> 0 us
  starting transfers between devices: 0.58 us -> 25.2 us
  other arithmetic: 4.53 us -> 19.4 us
  local copies, waits for them, and re-layouts: 5.35 us -> 12.4 us
    reduce_scatter x8 -> x0, waiting for transfers between devices: 275 us -> none  [the longest x3 121 us: shards(): lax.psum_scatter(term, 'expert', scatter_dimension=0, tiled=True)]
    ppermute x0 -> x17, waiting for transfers between devices: none -> 80.6 us  [the longest x10 63.2 us: swapped(): return lax.ppermute(block, axis, [(i, i ^ distance) for i in range(count)])]
    all_to_all x2 -> x0, blocking collectives: 68.3 us -> none  [the longest x1 36.3 us: shards(): lax.all_to_all(both_share[:slot_count].reshape(experts, capacity, width),...]
    ppermute x0 -> x17, starting transfers between devices: none -> 25 us  [the longest x6 13.1 us: shifted(): lax.ppermute(block, axis, [(i, (i + distance) % count) for i in range(cou...]
    all_gather x1 -> x0, blocking collectives: 14.2 us -> none  [shards(): pair_local = lax.all_gather(local, 'dp', axis=0, tiled=True)]
    broadcast_in_dim x0 -> x3, other arithmetic: none -> 7.68 us  [the longest x1 2.58 us: shards(): up_share.astype(jnp.bfloat16)[None]]
    another operation x1 -> x5, other arithmetic: 0.14 us -> 5.77 us  [the longest x2 3.26 us: gather_parts(): jnp.stack([jnp.where(low_chip, block, far), jnp.where(low_chip, far, bloc...]
  transfers between devices with their start and end apart: 10 -> 20, of which waited for: 8 -> 7; matrix products, arithmetic and copies ran while one was open for 1% -> 13% of each run, Pallas kernels for 15% -> 34%
where the time goes in v2:
time: 249 us; the launch traced here: 245 us
  Pallas kernels  91.1 us (37%)
  waiting for transfers between devices  80.6 us (32%)
  starting transfers between devices  25.2 us (10%)
  other arithmetic  19.4 us (8%)
  between operations  14 us (6%)
  local copies, waits for them, and re-layouts  12.4 us (5%)
  matrix products  2.5 us (1%)
    ppermute x10, waiting for transfers between devices, swapped(): return lax.ppermute(block, axis, [(i, i ^ distance) for i in range(count)])  63.2 us
    pallas_call x3, Pallas kernels, expand(): call(expand_body, grid=(row_blocks * col_blocks,), in_specs=[pl.BlockSpec...  23 us
    pallas_call x2, Pallas kernels, swiglu_steps(): call(functools.partial(swiglu_body, parts - 1, hidden_first), grid=(parts...  19.2 us
    ppermute x6, waiting for transfers between devices, shifted(): lax.ppermute(block, axis, [(i, (i + distance) % count) for i in range(cou...  17.4 us
    pallas_call x1, Pallas kernels, gate_up_values(): call(gate_up_body, grid=(parts,), in_specs=[pl.BlockSpec((1, rows, width)...  17.1 us
    pallas_call x2, Pallas kernels, back(): call(back_body, grid=(parts,), in_specs=[whole, whole, weight, weight], o...  14.3 us
    ppermute x6, starting transfers between devices, shifted(): lax.ppermute(block, axis, [(i, (i + distance) % count) for i in range(cou...  13.1 us
    ppermute x10, starting transfers between devices, swapped(): return lax.ppermute(block, axis, [(i, i ^ distance) for i in range(count)])  11.2 us
  transfers between devices with their start and end apart: 20, of which 7 were waited for; matrix products, arithmetic and copies ran while one was open for 13% of the time, Pallas kernels for 34%

profile of v2, /device:TPU:0, one launch (start us, length us, event | category | flops | bytes accessed | tf_op | source)
XLA Modules:
  0.0 245.2 jit_solution(17853545853741055886)
XLA Ops:
  14.0 3.1 %collective-permute-start.3 = (bf16[80,1792]{1,0:T(8,128)(2,1)S(1)}, bf16[80,1792]{1,0:T(8,128)(2,1)S(1)}, u32[]{:S(2)}, u32[]{:S(2)}) collective-permute-start(bf16[80,1792]{1,0:T(8,128)(2,1)S(1)} %get-tuple-element.34), channel_id=1, source_target_pairs={{0,4},{4,8},{8,12},{12,0},{1,5},{5,9},{9,13},{13,1},{2,6},{6,10},{... | collective-permute-start | bytes 860168 | tf_op jit(solution)/shard_map/ppermute | solution.py:290
  17.1 2.6 %collective-permute-start.4 = (bf16[80,1792]{1,0:T(8,128)(2,1)S(1)}, bf16[80,1792]{1,0:T(8,128)(2,1)S(1)}, u32[]{:S(2)}, u32[]{:S(2)}) collective-permute-start(bf16[80,1792]{1,0:T(8,128)(2,1)S(1)} %get-tuple-element.36), channel_id=1, source_target_pairs={{0,8},{4,12},{8,0},{12,4},{1,9},{5,13},{9,1},{13,5},{2,10},{6,14},... | collective-permute-start | bytes 860168 | tf_op jit(solution)/shard_map/ppermute | solution.py:290
  21.0 5.9 %collective-permute-done.3 = bf16[80,1792]{1,0:T(8,128)(2,1)S(1)} collective-permute-done((bf16[80,1792]{1,0:T(8,128)(2,1)S(1)}, bf16[80,1792]{1,0:T(8,128)(2,1)S(1)}, u32[]{:S(2)}, u32[]{:S(2)}) %collective-permute-start.3) | collective-permute-done | bytes 286752 | tf_op jit(solution)/shard_map/ppermute | solution.py:290
  26.9 11.5 %collective-permute-done.4 = bf16[80,1792]{1,0:T(8,128)(2,1)S(1)} collective-permute-done((bf16[80,1792]{1,0:T(8,128)(2,1)S(1)}, bf16[80,1792]{1,0:T(8,128)(2,1)S(1)}, u32[]{:S(2)}, u32[]{:S(2)}) %collective-permute-start.4) | collective-permute-done | bytes 286752 | tf_op jit(solution)/shard_map/ppermute | solution.py:290
  41.6 37.6 %collective-permute-done.6 = bf16[320,1792]{1,0:T(8,128)(2,1)} collective-permute-done((bf16[320,1792]{1,0:T(8,128)(2,1)S(1)}, bf16[320,1792]{1,0:T(8,128)(2,1)}, u32[]{:S(2)}, u32[]{:S(2)}) %collective-permute-start.6) | collective-permute-done | bytes 1146912 | tf_op jit(solution)/shard_map/ppermute | solution.py:285
  79.2 1.7 select_bitcast_fusion.3
  82.5 7.7 %shard_map.182.gate_ref = bf16[3584,640]{1,0:T(8,128)(2,1)} custom-call(bf16[1792,640]{1,0:T(8,128)(2,1)} %bitcast.68, s32[224,640]{1,0:T(8,128)} %bitcast.73), custom_call_target="tpu_custom_call" | custom-call | flops 4000000000 | bytes 30000000 | tf_op jit(solution)/shard_map/pallas_call | solution.py:85
  90.2 7.8 %shard_map.183.up_ref = bf16[3584,640]{1,0:T(8,128)(2,1)} custom-call(bf16[1792,640]{1,0:T(8,128)(2,1)} %bitcast.69, s32[224,640]{1,0:T(8,128)} %bitcast.75), custom_call_target="tpu_custom_call" | custom-call | flops 4000000000 | bytes 30000000 | tf_op jit(solution)/shard_map/pallas_call | solution.py:85
  98.0 7.5 %shard_map.184.down_ref = bf16[640,3584]{1,0:T(8,128)(2,1)} custom-call(bf16[320,3584]{1,0:T(8,128)(2,1)} %bitcast.70, s32[40,3584]{1,0:T(8,128)} %bitcast.71), custom_call_target="tpu_custom_call" | custom-call | flops 4000000000 | bytes 30000000 | tf_op jit(solution)/shard_map/pallas_call | solution.py:85
  105.5 1.9 select_bitcast_fusion.1
  107.8 2.4 copy.37
  110.3 11.4 %shard_map.185 = (bf16[320,640]{1,0:T(8,128)(2,1)}, bf16[320,640]{1,0:T(8,128)(2,1)}, bf16[320,640]{1,0:T(8,128)(2,1)}) custom-call(bf16[4,320,1792]{2,1,0:T(8,128)(2,1)} %bitcast.56, bf16[4,320,1792]{2,1,0:T(8,128)(2,1)} %bitcast.57, bf16[3584,640]{1,0:T(8,128)(2,1)} %shard_map.182.gate_ref, bf16[3584,640]{1,0:T(8,128)(2,1)} %shard_map.183.up_ref, ...), custom_call_target="tpu_custom_call" | custom-call | flops 4404019200 | bytes 20000000 | tf_op jit(solution)/shard_map/pallas_call | solution.py:144
  121.7 9.3 %shard_map.188 = bf16[320,3584]{1,0:T(8,128)(2,1)} custom-call(bf16[320,640]{1,0:T(8,128)(2,1)} %get-tuple-element.24.hidden_ref, bf16[4,320,1792]{2,1,0:T(8,128)(2,1)} %bitcast.58, s32[40,3584]{1,0:T(8,128)} %bitcast.72), custom_call_target="tpu_custom_call" | custom-call | flops 2936012800 | bytes 20000000 | tf_op jit(solution)/shard_map/pallas_call | solution.py:218
  132.3 1.7 collective-permute-start.15
  134.0 8.2 %shard_map.186 = bf16[4,320,896]{2,1,0:T(8,128)(2,1)} custom-call(bf16[320,640]{1,0:T(8,128)(2,1)} %get-tuple-element.20.gate_grad_ref, bf16[320,640]{1,0:T(8,128)(2,1)} %get-tuple-element.21.up_grad_ref, bf16[3584,640]{1,0:T(8,128)(2,1)} %shard_map.182.gate_ref, bf16[3584,640]{1,0:T(8,128)(2,1)} %shard_map.183.up_ref), custom_call_target="tpu_custom_call" | custom-call | flops 2936012800 | bytes 20000000 | tf_op jit(solution)/shard_map/pallas_call | solution.py:174
  143.9 7.8 %shard_map.180 = (bf16[256,384]{1,0:T(8,128)(2,1)}, bf16[256,384]{1,0:T(8,128)(2,1)}, bf16[256,384]{1,0:T(8,128)(2,1)}) custom-call(bf16[4,256,1792]{2,1,0:T(8,128)(2,1)} %bitcast.62, bf16[4,256,1792]{2,1,0:T(8,128)(2,1)} %bitcast.63, bf16[3584,384]{1,0:T(8,128)(2,1)} %gate_ref.3, bf16[3584,384]{1,0:T(8,128)(2,1)} %up_ref.3, bf16[3584,384]{1,0:T(8,128)(2,1)} %down_ref.1), custom_call_target="tpu_custom_call" | custom-call | flops 2113929216 | bytes 20000000 | tf_op jit(solution)/shard_map/pallas_call | solution.py:144
  151.7 2.0 pad_maximum_fusion.3
  153.7 17.1 %shard_map.187 = (bf16[1792,640]{1,0:T(8,128)(2,1)}, bf16[1792,640]{1,0:T(8,128)(2,1)}) custom-call(bf16[4,320,1792]{2,1,0:T(8,128)(2,1)} %bitcast.59, bf16[320,640]{1,0:T(8,128)(2,1)} %get-tuple-element.20.gate_grad_ref, bf16[320,640]{1,0:T(8,128)(2,1)} %get-tuple-element.21.up_grad_ref, s32[224,640]{1,0:T(8,128)} %bitcast.74, s32[224,640]{1,0:T(8,128)} %bitcast.76), custom_call_target="tpu_custom_call" | custom-call | flops 5872025600 | bytes 20000000 | tf_op jit(solution)/shard_map/pallas_call | solution.py:198
  172.9 1.7 collective-permute-start.13
  176.1 6.1 %shard_map.181 = bf16[4,256,896]{2,1,0:T(8,128)(2,1)} custom-call(bf16[256,384]{1,0:T(8,128)(2,1)} %get-tuple-element.18.gate_grad_ref, bf16[256,384]{1,0:T(8,128)(2,1)} %get-tuple-element.19.up_grad_ref, bf16[3584,384]{1,0:T(8,128)(2,1)} %gate_ref.3, bf16[3584,384]{1,0:T(8,128)(2,1)} %up_ref.3), custom_call_target="tpu_custom_call" | custom-call | flops 1409286144 | bytes 20000000 | tf_op jit(solution)/shard_map/pallas_call | solution.py:174
  183.8 2.5 %collective-permute-start.9 = (bf16[320,896]{1,0:T(8,128)(2,1)S(1)}, bf16[320,896]{1,0:T(8,128)(2,1)S(1)}, u32[]{:S(2)}, u32[]{:S(2)}) collective-permute-start(bf16[320,896]{1,0:T(8,128)(2,1)S(1)} %dynamic-slice_bitcast_fusion.2), channel_id=1, source_target_pairs={{0,2},{1,3},{2,0},{3,1},{4,6},{5,7},{6,4},{7,5},{8,10},{9,11},{10,... | collective-permute-start | bytes 1720328 | tf_op jit(solution)/shard_map/ppermute | solution.py:285
  186.3 2.6 %fusion.4 = bf16[1,320,1792]{2,1,0:T(8,128)(2,1)} fusion(bf16[320,1792]{1,0:T(8,128)(2,1)} %collective-permute-done.15, bf16[320,3584]{1,0:T(8,128)(2,1)S(1)} %copy-done.5, s32[]{:T(128)S(6)} %select_n.125), kind=kLoop, calls=%fused_computation.19 | loop fusion | flops 2293760 | bytes 3440644 | tf_op jit(solution)/shard_map/broadcast_in_dim | solution.py:409
  188.8 11.7 %collective-permute-done.14 = bf16[896,640]{1,0:T(8,128)(2,1)} collective-permute-done((bf16[896,640]{1,0:T(8,128)(2,1)S(1)}, bf16[896,640]{1,0:T(8,128)(2,1)}, u32[]{:S(2)}, u32[]{:S(2)}) %collective-permute-start.14) | collective-permute-done | bytes 1146912 | tf_op jit(solution)/shard_map/ppermute | solution.py:285
  200.6 2.6 %fusion.3 = bf16[1,896,640]{2,1,0:T(8,128)(2,1)} fusion(bf16[896,640]{1,0:T(8,128)(2,1)} %collective-permute-done.14, bf16[1792,640]{1,0:T(8,128)(2,1)S(1)} %copy-done.6, s32[]{:T(128)S(6)} %select_n.123), kind=kLoop, calls=%fused_computation.18 | loop fusion | flops 2293760 | bytes 3440644 | tf_op jit(solution)/shard_map/broadcast_in_dim | solution.py:408
  203.4 2.5 %collective-permute-start.1 = (bf16[256,896]{1,0:T(8,128)(2,1)S(1)}, bf16[256,896]{1,0:T(8,128)(2,1)S(1)}, u32[]{:S(2)}, u32[]{:S(2)}) collective-permute-start(bf16[256,896]{1,0:T(8,128)(2,1)S(1)} %dynamic-slice_bitcast_fusion.3), channel_id=1, source_target_pairs={{0,2},{1,3},{2,0},{3,1},{4,6},{5,7},{6,4},{7,5},{8,10},{9,11},{10,... | collective-permute-start | bytes 1376264 | tf_op jit(solution)/shard_map/ppermute | solution.py:285
  206.2 3.1 %collective-permute-start.10 = (bf16[80,896]{1,0:T(8,128)(2,1)S(1)}, bf16[80,896]{1,0:T(8,128)(2,1)S(1)}, u32[]{:S(2)}, u32[]{:S(2)}) collective-permute-start(bf16[80,896]{1,0:T(8,128)(2,1)S(1)} %get-tuple-element.40), channel_id=1, source_target_pairs={{0,12},{4,0},{8,4},{12,8},{1,13},{5,1},{9,5},{13,9},{2,14},{6,2},{... | collective-permute-start | bytes 430088 | tf_op jit(solution)/shard_map/ppermute | solution.py:290
  209.3 3.0 %collective-permute-start.11 = (bf16[80,896]{1,0:T(8,128)(2,1)S(1)}, bf16[80,896]{1,0:T(8,128)(2,1)S(1)}, u32[]{:S(2)}, u32[]{:S(2)}) collective-permute-start(bf16[80,896]{1,0:T(8,128)(2,1)S(1)} %get-tuple-element.39), channel_id=1, source_target_pairs={{0,8},{4,12},{8,0},{12,4},{1,9},{5,13},{9,1},{13,5},{2,10},{6,14},... | collective-permute-start | bytes 430088 | tf_op jit(solution)/shard_map/ppermute | solution.py:290
  212.3 3.0 %collective-permute-done.1 = bf16[256,896]{1,0:T(8,128)(2,1)S(1)} collective-permute-done((bf16[256,896]{1,0:T(8,128)(2,1)S(1)}, bf16[256,896]{1,0:T(8,128)(2,1)S(1)}, u32[]{:S(2)}, u32[]{:S(2)}) %collective-permute-start.1) | collective-permute-done | bytes 458784 | tf_op jit(solution)/shard_map/ppermute | solution.py:285
  215.9 9.3 %collective-permute-done.13 = bf16[896,640]{1,0:T(8,128)(2,1)} collective-permute-done((bf16[896,640]{1,0:T(8,128)(2,1)S(1)}, bf16[896,640]{1,0:T(8,128)(2,1)}, u32[]{:S(2)}, u32[]{:S(2)}) %collective-permute-start.13) | collective-permute-done | bytes 1146912 | tf_op jit(solution)/shard_map/ppermute | solution.py:285
  225.1 2.5 %fusion.2 = bf16[1,896,640]{2,1,0:T(8,128)(2,1)} fusion(bf16[896,640]{1,0:T(8,128)(2,1)} %collective-permute-done.13, bf16[1792,640]{1,0:T(8,128)(2,1)S(1)} %copy-done.4, s32[]{:T(128)S(6)} %select_n.123), kind=kLoop, calls=%fused_computation.17 | loop fusion | flops 2293760 | bytes 3440644 | tf_op jit(solution)/shard_map/broadcast_in_dim | solution.py:407
  227.7 1.6 collective-permute-done.2
  230.3 8.3 %shard_map.189 = (bf16[896,384]{1,0:T(8,128)(2,1)}, bf16[896,384]{1,0:T(8,128)(2,1)}, bf16[896,384]{1,0:T(8,128)(2,1)}) custom-call(bf16[1,1024,1792]{2,1,0:T(8,128)(2,1)} %bitcast.60, bf16[1,1024,1792]{2,1,0:T(8,128)(2,1)} %bitcast.61, bf16[1024,1152]{1,0:T(8,128)(2,1)} %all-gather.6.cloned.1.call-done.steps_ref), custom_call_target="tpu_custom_call" | custom-call | flops 2113929216 | bytes 20000000 | tf_op jit(solution)/shard_map/pallas_call | solution.py:248
  (80 shorter events, 23.6 us)
Async XLA Ops:
  7.2 136.7 %all-gather.8.cloned.1.call-start = ((), (), s32[]{:S(2)}) async-start(), calls=%async_computation.1 | async-start | bytes 4128768 | tf_op jit(solution)/shard_map/all_gather | solution.py:363
  9.1 0.8 copy-start.2
  9.9 220.4 %all-gather.10.cloned.1.call-start = ((), (), s32[]{:S(2)}) async-start(), calls=%async_computation.2 | async-start | bytes 4128768 | tf_op jit(solution)/shard_map/all_gather | solution.py:395
  12.1 1.6 copy-start.8
  13.9 26.1 %copy-start.3 = (bf16[128,1792]{1,0:T(8,128)(2,1)S(1)}, bf16[128,1792]{1,0:T(8,128)(2,1)}, u32[]{:S(2)}) copy-start(bf16[128,1792]{1,0:T(8,128)(2,1)} %copy-done.2) | copy-start | bytes 1376260
  14.0 12.9 %collective-permute-start.3 = (bf16[80,1792]{1,0:T(8,128)(2,1)S(1)}, bf16[80,1792]{1,0:T(8,128)(2,1)S(1)}, u32[]{:S(2)}, u32[]{:S(2)}) collective-permute-start(bf16[80,1792]{1,0:T(8,128)(2,1)S(1)} %get-tuple-element.34), channel_id=1, source_target_pairs={{0,4},{4,8},{8,12},{12,0},{1,5},{5,9},{9,13},{13,1},{2,6},{6,10},{... | collective-permute-start | bytes 860168 | tf_op jit(solution)/shard_map/ppermute | solution.py:290
  17.1 21.3 %collective-permute-start.4 = (bf16[80,1792]{1,0:T(8,128)(2,1)S(1)}, bf16[80,1792]{1,0:T(8,128)(2,1)S(1)}, u32[]{:S(2)}, u32[]{:S(2)}) collective-permute-start(bf16[80,1792]{1,0:T(8,128)(2,1)S(1)} %get-tuple-element.36), channel_id=1, source_target_pairs={{0,8},{4,12},{8,0},{12,4},{1,9},{5,13},{9,1},{13,5},{2,10},{6,14},... | collective-permute-start | bytes 860168 | tf_op jit(solution)/shard_map/ppermute | solution.py:290
  19.7 18.7 %collective-permute-start.5 = (bf16[80,1792]{1,0:T(8,128)(2,1)S(1)}, bf16[80,1792]{1,0:T(8,128)(2,1)S(1)}, u32[]{:S(2)}, u32[]{:S(2)}) collective-permute-start(bf16[80,1792]{1,0:T(8,128)(2,1)S(1)} %get-tuple-element.35), channel_id=1, source_target_pairs={{0,12},{4,0},{8,4},{12,8},{1,13},{5,1},{9,5},{13,9},{2,14},{6,2},{... | collective-permute-start | bytes 860168 | tf_op jit(solution)/shard_map/ppermute | solution.py:290
  38.5 40.8 %collective-permute-start.6 = (bf16[320,1792]{1,0:T(8,128)(2,1)S(1)}, bf16[320,1792]{1,0:T(8,128)(2,1)}, u32[]{:S(2)}, u32[]{:S(2)}) collective-permute-start(bf16[320,1792]{1,0:T(8,128)(2,1)S(1)} %pad_maximum_fusion.2), channel_id=1, source_target_pairs={{0,2},{1,3},{2,0},{3,1},{4,6},{5,7},{6,4},{7,5},{8,10},{9,11},{10,... | collective-permute-start | bytes 3440648 | tf_op jit(solution)/shard_map/ppermute | solution.py:285
  40.1 0.7 collective-permute-start.16
  40.8 0.8 copy-start.7
  41.6 188.8 %all-gather.6.cloned.1.call-start = ((), (), s32[]{:S(2)}) async-start(), calls=%async_computation | async-start | bytes 2949120 | tf_op jit(solution)/shard_map/all_gather | solution.py:397
  82.5 23.0 %collective-permute-start.7 = (bf16[2,320,1792]{2,1,0:T(8,128)(2,1)}, bf16[2,320,1792]{2,1,0:T(8,128)(2,1)}, u32[]{:S(2)}, u32[]{:S(2)}) collective-permute-start(bf16[2,320,1792]{2,1,0:T(8,128)(2,1)} %pad_maximum_fusion.1), channel_id=1, source_target_pairs={{0,1},{1,0},{2,3},{3,2},{4,5},{5,4},{6,7},{7,6},{8,9},{9,8},{10,11... | collective-permute-start | bytes 6881288 | tf_op jit(solution)/shard_map/ppermute | solution.py:285
  132.3 54.0 %collective-permute-start.15 = (bf16[320,1792]{1,0:T(8,128)(2,1)S(1)}, bf16[320,1792]{1,0:T(8,128)(2,1)}, u32[]{:S(2)}, u32[]{:S(2)}) collective-permute-start(bf16[320,1792]{1,0:T(8,128)(2,1)S(1)} %constant_dynamic-slice_fusion), channel_id=1, source_target_pairs={{0,16},{16,0},{1,17},{17,1},{2,18},{18,2},{3,19},{19,3},{4,20},{20... | collective-permute-start | bytes 3440648 | tf_op jit(solution)/shard_map/ppermute | solution.py:285
  143.6 31.0 %collective-permute-start.8 = (bf16[2,320,896]{2,1,0:T(8,128)(2,1)S(1)}, bf16[2,320,896]{2,1,0:T(8,128)(2,1)}, u32[]{:S(2)}, u32[]{:S(2)}) collective-permute-start(bf16[2,320,896]{2,1,0:T(8,128)(2,1)S(1)} %dynamic-slice_bitcast_fusion), channel_id=1, source_target_pairs={{0,1},{1,0},{2,3},{3,2},{4,5},{5,4},{6,7},{7,6},{8,9},{9,8},{10,11... | collective-permute-start | bytes 3440648 | tf_op jit(solution)/shard_map/ppermute | solution.py:285
  170.8 2.0 copy-start.4
  170.8 3.8 %copy-start = (bf16[4,320,896]{2,1,0:T(8,128)(2,1)S(1)}, bf16[4,320,896]{2,1,0:T(8,128)(2,1)}, u32[]{:S(2)}) copy-start(bf16[4,320,896]{2,1,0:T(8,128)(2,1)} %shard_map.186) | copy-start | bytes 6881284
  172.3 28.3 %collective-permute-start.14 = (bf16[896,640]{1,0:T(8,128)(2,1)S(1)}, bf16[896,640]{1,0:T(8,128)(2,1)}, u32[]{:S(2)}, u32[]{:S(2)}) collective-permute-start(bf16[896,640]{1,0:T(8,128)(2,1)S(1)} %constant_dynamic-slice_fusion.1), channel_id=1, source_target_pairs={{0,16},{16,0},{1,17},{17,1},{2,18},{18,2},{3,19},{19,3},{4,20},{20... | collective-permute-start | bytes 3440648 | tf_op jit(solution)/shard_map/ppermute | solution.py:285
  172.9 52.3 %collective-permute-start.13 = (bf16[896,640]{1,0:T(8,128)(2,1)S(1)}, bf16[896,640]{1,0:T(8,128)(2,1)}, u32[]{:S(2)}, u32[]{:S(2)}) collective-permute-start(bf16[896,640]{1,0:T(8,128)(2,1)S(1)} %constant_dynamic-slice_fusion.2), channel_id=1, source_target_pairs={{0,16},{16,0},{1,17},{17,1},{2,18},{18,2},{3,19},{19,3},{4,20},{20... | collective-permute-start | bytes 3440648 | tf_op jit(solution)/shard_map/ppermute | solution.py:285
  182.2 4.1 %copy-start.5 = (bf16[320,3584]{1,0:T(8,128)(2,1)S(1)}, bf16[320,3584]{1,0:T(8,128)(2,1)}, u32[]{:S(2)}) copy-start(bf16[320,3584]{1,0:T(8,128)(2,1)} %shard_map.188) | copy-start | bytes 6881284
  183.6 19.5 %collective-permute-start = (bf16[2,256,896]{2,1,0:T(8,128)(2,1)S(1)}, bf16[2,256,896]{2,1,0:T(8,128)(2,1)S(1)}, u32[]{:S(2)}, u32[]{:S(2)}) collective-permute-start(bf16[2,256,896]{2,1,0:T(8,128)(2,1)S(1)} %dynamic-slice_bitcast_fusion.1), channel_id=1, source_target_pairs={{0,1},{1,0},{2,3},{3,2},{4,5},{5,4},{6,7},{7,6},{8,9},{9,8},{10,11... | collective-permute-start | bytes 2752520 | tf_op jit(solution)/shard_map/ppermute | solution.py:285
  183.8 16.8 %copy-start.6 = (bf16[1792,640]{1,0:T(8,128)(2,1)S(1)}, bf16[1792,640]{1,0:T(8,128)(2,1)}, u32[]{:S(2)}) copy-start(bf16[1792,640]{1,0:T(8,128)(2,1)} %get-tuple-element.23) | copy-start | bytes 6881284
  183.8 22.2 %collective-permute-start.9 = (bf16[320,896]{1,0:T(8,128)(2,1)S(1)}, bf16[320,896]{1,0:T(8,128)(2,1)S(1)}, u32[]{:S(2)}, u32[]{:S(2)}) collective-permute-start(bf16[320,896]{1,0:T(8,128)(2,1)S(1)} %dynamic-slice_bitcast_fusion.2), channel_id=1, source_target_pairs={{0,2},{1,3},{2,0},{3,1},{4,6},{5,7},{6,4},{7,5},{8,10},{9,11},{10,... | collective-permute-start | bytes 1720328 | tf_op jit(solution)/shard_map/ppermute | solution.py:285
  188.8 14.3 %copy-start.1 = (bf16[4,256,896]{2,1,0:T(8,128)(2,1)S(1)}, bf16[4,256,896]{2,1,0:T(8,128)(2,1)}, u32[]{:S(2)}) copy-start(bf16[4,256,896]{2,1,0:T(8,128)(2,1)} %shard_map.181) | copy-start | bytes 5505028
  203.4 11.9 %collective-permute-start.1 = (bf16[256,896]{1,0:T(8,128)(2,1)S(1)}, bf16[256,896]{1,0:T(8,128)(2,1)S(1)}, u32[]{:S(2)}, u32[]{:S(2)}) collective-permute-start(bf16[256,896]{1,0:T(8,128)(2,1)S(1)} %dynamic-slice_bitcast_fusion.3), channel_id=1, source_target_pairs={{0,2},{1,3},{2,0},{3,1},{4,6},{5,7},{6,4},{7,5},{8,10},{9,11},{10,... | collective-permute-start | bytes 1376264 | tf_op jit(solution)/shard_map/ppermute | solution.py:285
  206.2 21.5 %collective-permute-start.10 = (bf16[80,896]{1,0:T(8,128)(2,1)S(1)}, bf16[80,896]{1,0:T(8,128)(2,1)S(1)}, u32[]{:S(2)}, u32[]{:S(2)}) collective-permute-start(bf16[80,896]{1,0:T(8,128)(2,1)S(1)} %get-tuple-element.40), channel_id=1, source_target_pairs={{0,12},{4,0},{8,4},{12,8},{1,13},{5,1},{9,5},{13,9},{2,14},{6,2},{... | collective-permute-start | bytes 430088 | tf_op jit(solution)/shard_map/ppermute | solution.py:290
  209.3 18.4 %collective-permute-start.11 = (bf16[80,896]{1,0:T(8,128)(2,1)S(1)}, bf16[80,896]{1,0:T(8,128)(2,1)S(1)}, u32[]{:S(2)}, u32[]{:S(2)}) collective-permute-start(bf16[80,896]{1,0:T(8,128)(2,1)S(1)} %get-tuple-element.39), channel_id=1, source_target_pairs={{0,8},{4,12},{8,0},{12,4},{1,9},{5,13},{9,1},{13,5},{2,10},{6,14},... | collective-permute-start | bytes 430088 | tf_op jit(solution)/shard_map/ppermute | solution.py:290
  212.3 15.4 %collective-permute-start.12 = (bf16[80,896]{1,0:T(8,128)(2,1)S(1)}, bf16[80,896]{1,0:T(8,128)(2,1)S(1)}, u32[]{:S(2)}, u32[]{:S(2)}) collective-permute-start(bf16[80,896]{1,0:T(8,128)(2,1)S(1)} %get-tuple-element.38), channel_id=1, source_target_pairs={{0,4},{4,8},{8,12},{12,0},{1,5},{5,9},{9,13},{13,1},{2,6},{6,10},{... | collective-permute-start | bytes 430088 | tf_op jit(solution)/shard_map/ppermute | solution.py:290
  215.5 13.8 %collective-permute-start.2 = (bf16[128,896]{1,0:T(8,128)(2,1)S(1)}, bf16[128,896]{1,0:T(8,128)(2,1)S(1)}, u32[]{:S(2)}, u32[]{:S(2)}) collective-permute-start(bf16[128,896]{1,0:T(8,128)(2,1)S(1)} %constant_dynamic-slice_fusion.3), channel_id=1, source_target_pairs={{0,16},{16,0},{1,17},{17,1},{2,18},{18,2},{3,19},{19,3},{4,20},{20... | collective-permute-start | bytes 688136 | tf_op jit(solution)/shard_map/ppermute | solution.py:285
Sparse Core Ops, SparseCore 0:
  10.5 42.0 all-gather.7
  55.0 49.4 all-gather.9
  153.8 52.7 all-gather.5

commit v3 on v2

--- a/solution.py
+++ b/solution.py
@@ -290,34 +290,43 @@
     return lax.ppermute(block, axis, [(i, (i + distance) % count) for i in range(count)])
 
 
-def gather_parts(block):
+def gather_parts(block, beside):
     if lax.axis_size("tensor") != 4:
-        return lax.all_gather(block, "tensor", axis=0)
+        return lax.all_gather(block, "tensor", axis=0), beside
     place = lax.axis_index("tensor")
     low_chip, low_core = place // 2 == 0, place % 2 == 0
-    far = swapped(block, "tensor", 2)
+    far, beside = lax.optimization_barrier((swapped(block, "tensor", 2), beside))
     mine = jnp.stack([jnp.where(low_chip, block, far), jnp.where(low_chip, far, block)])
     near = swapped(mine, "tensor", 1)
     both = jnp.stack([jnp.where(low_core, mine, near), jnp.where(low_core, near, mine)], axis=1)
-    return both.reshape((4,) + block.shape)
+    return both.reshape((4,) + block.shape), beside
+
+
+def gather_groups(block):
+    count, rows = lax.axis_size("expert"), block.shape[0]
+    arrived = [shifted(block, "expert", k) for k in range(count - 1, 0, -1)] + [block]
+    start = (count - 1 - lax.axis_index("expert")) * rows
+    return lax.dynamic_slice_in_dim(jnp.concatenate(arrived + arrived, axis=0), start, count * rows, 0)
 
 
 def added(a, b):
     return a.astype(jnp.float32) + b.astype(jnp.float32)
 
 
-def scatter_parts(parts):
+def scatter_parts(parts, later=()):
     if lax.axis_size("tensor") != 4:
-        return lax.psum_scatter(parts, "tensor", scatter_dimension=0, tiled=True)[0].astype(jnp.float32)
+        total = lax.psum_scatter(parts, "tensor", scatter_dimension=0, tiled=True)[0]
+        return total.astype(jnp.float32), later
     place = lax.axis_index("tensor")
     chip, core = place // 2, place % 2
     split = parts.reshape((2, 2) + parts.shape[1:])
     send = lax.dynamic_index_in_dim(split, 1 - core, 1, keepdims=False)
     keep = lax.dynamic_index_in_dim(split, core, 1, keepdims=False)
-    summed = added(keep, swapped(send, "tensor", 1)).astype(jnp.bfloat16)
+    near, later = lax.optimization_barrier((swapped(send, "tensor", 1), later))
+    summed = added(keep, near).astype(jnp.bfloat16)
     send = lax.dynamic_index_in_dim(summed, 1 - chip, 0, keepdims=False)
     keep = lax.dynamic_index_in_dim(summed, chip, 0, keepdims=False)
-    return added(keep, swapped(send, "tensor", 2))
+    return added(keep, swapped(send, "tensor", 2)), later
 
 
 def scatter_batches(block, axis):
@@ -358,7 +367,7 @@
     ).astype(jnp.bfloat16)
     blocks = [slot_local[k * capacity : (k + 1) * capacity] for k in range(experts)]
     arrived = [blocks[0]] + [shifted(blocks[k], "expert", k) for k in range(1, experts)]
-    slot_both = gather_parts(jnp.concatenate(arrived, axis=0))
+    slots = jnp.concatenate(arrived, axis=0)
 
     pair_both = lax.all_gather(local, ("tensor", "dp"), axis=0).reshape(
         parts, dp_count * tok_count, 2 * width
@@ -371,15 +380,20 @@
     res_hidden, res_gate_step, res_up_step = swiglu_steps(pair_both, res_gate, res_up, res_down, False)
     res_back = back(res_gate_step, res_up_step, res_gate, res_up, parts)
 
+    slot_both, (gate_dense, up_dense, down_dense) = gather_parts(slots, (gate_dense, up_dense, down_dense))
+    slot_both, res_hidden, res_gate_step, res_up_step, res_back = lax.optimization_barrier(
+        (slot_both, res_hidden, res_gate_step, res_up_step, res_back)
+    )
     hidden, gate_grad, up_grad = swiglu_steps(slot_both, gate_dense, up_dense, down_dense, True)
     slot_back = back(gate_grad, up_grad, gate_dense, up_dense, parts)
+    slot_back, hidden = lax.optimization_barrier((slot_back, hidden))
+    down_terms = down_values_of(slot_both, hidden, down_words[0])
+    slot_share, (down_terms, gate_grad, up_grad) = scatter_parts(slot_back, (down_terms, gate_grad, up_grad))
     gate_terms, up_terms = gate_up_values(slot_both, gate_grad, up_grad, gate_words[0], up_words[0])
-    down_terms = down_values_of(slot_both, hidden, down_words[0])
-
-    slot_share = scatter_parts(slot_back).astype(jnp.bfloat16)
+    slot_share = slot_share.astype(jnp.bfloat16)
     blocks = [slot_share[k * capacity : (k + 1) * capacity] for k in range(experts)]
     returned = [blocks[0]] + [shifted(blocks[k], "expert", -k) for k in range(1, experts)]
-    res_share = scatter_batches(scatter_parts(res_back).astype(jnp.bfloat16), 0)
+    res_share = scatter_batches(scatter_parts(res_back)[0].astype(jnp.bfloat16), 0)
     combined = res_share + mm(taken, jnp.concatenate(returned, axis=0), (0, 0))
 
     gate_share = scatter_batches(gate_terms, 0)
@@ -394,7 +408,7 @@
         )
         all_rows = lax.all_gather(turned, ("tensor", "dp"), axis=0).reshape(1, -1, 2 * width)
         steps = jnp.concatenate([res_gate_step, res_up_step, res_hidden], axis=1)
-        steps = lax.all_gather(steps, "expert", axis=0, tiled=True)
+        steps = gather_groups(steps)
         res_sums = weight_grads(all_rows, steps)
     else:
         steps = jnp.concatenate([res_gate_step, res_up_step, res_hidden], axis=1)

time: 249 us -> 307 us (1.23)
  waiting for transfers between devices: 80.6 us -> 112 us
  starting transfers between devices: 25.2 us -> 43.5 us
  local copies, waits for them, and re-layouts: 12.4 us -> 23.2 us
    ppermute x6 -> x9, waiting for transfers between devices: 17.4 us -> 36.9 us  [shifted(): lax.ppermute(block, axis, [(i, (i + distance) % count) for i in range(cou...]
    ppermute x6 -> x9, starting transfers between devices: 13.1 us -> 29.3 us  [shifted(): lax.ppermute(block, axis, [(i, (i + distance) % count) for i in range(cou...]
    ppermute x10, waiting for transfers between devices: 63.2 us -> 75 us  [swapped(): return lax.ppermute(block, axis, [(i, i ^ distance) for i in range(count)])]
    unnamed x19 -> x56, local copies, waits for them, and re-layouts: 2.58 us -> 6.89 us
    dynamic_slice x0 -> x1, local copies, waits for them, and re-layouts: none -> 3.25 us  [gather_groups(): lax.dynamic_slice_in_dim(jnp.concatenate(arrived + arrived, axis=0), star...]
  transfers between devices with their start and end apart: 20 -> 22, of which waited for: 7 -> 6; matrix products, arithmetic and copies ran while one was open for 13% -> 12% of each run, Pallas kernels for 34% -> 30%
where the time goes in v3:
time: 307 us; the launch traced here: 306 us
  waiting for transfers between devices  112 us (36%)
  Pallas kernels  91 us (30%)
  starting transfers between devices  43.5 us (14%)
  local copies, waits for them, and re-layouts  23.2 us (8%)
  other arithmetic  18.4 us (6%)
  between operations  14.5 us (5%)
  matrix products  3.63 us (1%)
    ppermute x10, waiting for transfers between devices, swapped(): return lax.ppermute(block, axis, [(i, i ^ distance) for i in range(count)])  75 us
    ppermute x9, waiting for transfers between devices, shifted(): lax.ppermute(block, axis, [(i, (i + distance) % count) for i in range(cou...  36.9 us
    ppermute x9, starting transfers between devices, shifted(): lax.ppermute(block, axis, [(i, (i + distance) % count) for i in range(cou...  29.3 us
    pallas_call x3, Pallas kernels, expand(): call(expand_body, grid=(row_blocks * col_blocks,), in_specs=[pl.BlockSpec...  22.7 us
    pallas_call x2, Pallas kernels, swiglu_steps(): call(functools.partial(swiglu_body, parts - 1, hidden_first), grid=(parts...  19.3 us
    pallas_call x1, Pallas kernels, gate_up_values(): call(gate_up_body, grid=(parts,), in_specs=[pl.BlockSpec((1, rows, width)...  16.9 us
    pallas_call x2, Pallas kernels, back(): call(back_body, grid=(parts,), in_specs=[whole, whole, weight, weight], o...  14.5 us
    ppermute x10, starting transfers between devices, swapped(): return lax.ppermute(block, axis, [(i, i ^ distance) for i in range(count)])  13.4 us
  transfers between devices with their start and end apart: 22, of which 6 were waited for; matrix products, arithmetic and copies ran while one was open for 12% of the time, Pallas kernels for 30%

profile of v3, /device:TPU:0, one launch (start us, length us, event | category | flops | bytes accessed | tf_op | source)
XLA Modules:
  0.0 306.1 jit_solution(3721978518452129628)
XLA Ops:
  14.0 5.1 %collective-permute-start.2 = (bf16[80,1792]{1,0:T(8,128)(2,1)S(1)}, bf16[80,1792]{1,0:T(8,128)(2,1)S(1)}, u32[]{:S(2)}, u32[]{:S(2)}) collective-permute-start(bf16[80,1792]{1,0:T(8,128)(2,1)S(1)} %get-tuple-element.65), channel_id=1, source_target_pairs={{0,12},{4,0},{8,4},{12,8},{1,13},{5,1},{9,5},{13,9},{2,14},{6,2},{... | collective-permute-start | bytes 860168 | tf_op jit(solution)/shard_map/ppermute | solution.py:290
  20.1 6.3 %collective-permute-done.2 = bf16[80,1792]{1,0:T(8,128)(2,1)S(1)} collective-permute-done((bf16[80,1792]{1,0:T(8,128)(2,1)S(1)}, bf16[80,1792]{1,0:T(8,128)(2,1)S(1)}, u32[]{:S(2)}, u32[]{:S(2)}) %collective-permute-start.2) | collective-permute-done | bytes 286752 | tf_op jit(solution)/shard_map/ppermute | solution.py:290
  26.4 17.1 %collective-permute-done.1 = bf16[80,1792]{1,0:T(8,128)(2,1)S(1)} collective-permute-done((bf16[80,1792]{1,0:T(8,128)(2,1)S(1)}, bf16[80,1792]{1,0:T(8,128)(2,1)S(1)}, u32[]{:S(2)}, u32[]{:S(2)}) %collective-permute-start.1) | collective-permute-done | bytes 286752 | tf_op jit(solution)/shard_map/ppermute | solution.py:290
  45.2 7.6 %shard_map.180.gate_ref = bf16[3584,640]{1,0:T(8,128)(2,1)} custom-call(bf16[1792,640]{1,0:T(8,128)(2,1)} %bitcast.68, s32[224,640]{1,0:T(8,128)} %bitcast.73), custom_call_target="tpu_custom_call" | custom-call | flops 4000000000 | bytes 30000000 | tf_op jit(solution)/shard_map/pallas_call | solution.py:85
  52.8 7.6 %shard_map.181.up_ref = bf16[3584,640]{1,0:T(8,128)(2,1)} custom-call(bf16[1792,640]{1,0:T(8,128)(2,1)} %bitcast.69, s32[224,640]{1,0:T(8,128)} %bitcast.75), custom_call_target="tpu_custom_call" | custom-call | flops 4000000000 | bytes 30000000 | tf_op jit(solution)/shard_map/pallas_call | solution.py:85
  60.4 7.5 %shard_map.182.down_ref = bf16[640,3584]{1,0:T(8,128)(2,1)} custom-call(bf16[320,3584]{1,0:T(8,128)(2,1)} %bitcast.70, s32[40,3584]{1,0:T(8,128)} %bitcast.71), custom_call_target="tpu_custom_call" | custom-call | flops 4000000000 | bytes 30000000 | tf_op jit(solution)/shard_map/pallas_call | solution.py:85
  67.9 2.8 collective-permute-done.3
  70.7 1.7 select_bitcast_fusion.3
  75.5 3.2 %collective-permute-done.4 = bf16[2,320,1792]{2,1,0:T(8,128)(2,1)} collective-permute-done((bf16[2,320,1792]{2,1,0:T(8,128)(2,1)}, bf16[2,320,1792]{2,1,0:T(8,128)(2,1)}, u32[]{:S(2)}, u32[]{:S(2)}) %collective-permute-start.4) | collective-permute-done | bytes 2293792 | tf_op jit(solution)/shard_map/ppermute | solution.py:285
  78.8 1.9 select_bitcast_fusion.1
  81.1 2.4 copy.36
  83.6 7.8 %shard_map.183 = (bf16[256,384]{1,0:T(8,128)(2,1)}, bf16[256,384]{1,0:T(8,128)(2,1)}, bf16[256,384]{1,0:T(8,128)(2,1)}) custom-call(bf16[4,256,1792]{2,1,0:T(8,128)(2,1)} %bitcast.62, bf16[4,256,1792]{2,1,0:T(8,128)(2,1)} %bitcast.63, bf16[3584,384]{1,0:T(8,128)(2,1)} %gate_ref.3, bf16[3584,384]{1,0:T(8,128)(2,1)} %up_ref.3, bf16[3584,384]{1,0:T(8,128)(2,1)} %down_ref.1), custom_call_target="tpu_custom_call" | custom-call | flops 2113929216 | bytes 20000000 | tf_op jit(solution)/shard_map/pallas_call | solution.py:144
  91.3 6.3 %shard_map.184 = bf16[4,256,896]{2,1,0:T(8,128)(2,1)} custom-call(bf16[256,384]{1,0:T(8,128)(2,1)} %get-tuple-element.53.gate_grad_ref, bf16[256,384]{1,0:T(8,128)(2,1)} %get-tuple-element.54.up_grad_ref, bf16[3584,384]{1,0:T(8,128)(2,1)} %gate_ref.3, bf16[3584,384]{1,0:T(8,128)(2,1)} %up_ref.3), custom_call_target="tpu_custom_call" | custom-call | flops 1409286144 | bytes 20000000 | tf_op jit(solution)/shard_map/pallas_call | solution.py:174
  97.7 16.6 %collective-permute-start.17 = (bf16[256,1152]{1,0:T(8,128)(2,1)S(1)}, bf16[256,1152]{1,0:T(8,128)(2,1)S(1)}, u32[]{:S(2)}, u32[]{:S(2)}) collective-permute-start(bf16[256,1152]{1,0:T(8,128)(2,1)S(1)} %constant_dynamic-update-slice_fusion.2), channel_id=1, source_target_pairs={{0,12},{4,0},{8,4},{12,8},{1,13},{5,1},{9,5},{13,9},{2,14},{6,2},{... | collective-permute-start | bytes 1769480 | tf_op jit(solution)/shard_map/ppermute | solution.py:290
  114.4 4.6 %collective-permute-start.18 = (bf16[256,1152]{1,0:T(8,128)(2,1)S(1)}, bf16[256,1152]{1,0:T(8,128)(2,1)S(1)}, u32[]{:S(2)}, u32[]{:S(2)}) collective-permute-start(bf16[256,1152]{1,0:T(8,128)(2,1)S(1)} %constant_dynamic-update-slice_fusion.2), channel_id=1, source_target_pairs={{0,8},{4,12},{8,0},{12,4},{1,9},{5,13},{9,1},{13,5},{2,10},{6,14},... | collective-permute-start | bytes 1769480 | tf_op jit(solution)/shard_map/ppermute | solution.py:290
  119.0 1.9 collective-permute-start.19
  122.5 2.1 collective-permute-start.5
  124.5 11.5 %shard_map.185 = (bf16[320,640]{1,0:T(8,128)(2,1)}, bf16[320,640]{1,0:T(8,128)(2,1)}, bf16[320,640]{1,0:T(8,128)(2,1)}) custom-call(bf16[4,320,1792]{2,1,0:T(8,128)(2,1)} %bitcast.56, bf16[4,320,1792]{2,1,0:T(8,128)(2,1)} %bitcast.57, bf16[3584,640]{1,0:T(8,128)(2,1)} %shard_map.180.gate_ref, bf16[3584,640]{1,0:T(8,128)(2,1)} %shard_map.181.up_ref, ...), custom_call_target="tpu_custom_call" | custom-call | flops 4404019200 | bytes 20000000 | tf_op jit(solution)/shard_map/pallas_call | solution.py:144
  136.1 8.2 %shard_map.186 = bf16[4,320,896]{2,1,0:T(8,128)(2,1)} custom-call(bf16[320,640]{1,0:T(8,128)(2,1)} %get-tuple-element.48.gate_grad_ref, bf16[320,640]{1,0:T(8,128)(2,1)} %get-tuple-element.49.up_grad_ref, bf16[3584,640]{1,0:T(8,128)(2,1)} %shard_map.180.gate_ref, bf16[3584,640]{1,0:T(8,128)(2,1)} %shard_map.181.up_ref), custom_call_target="tpu_custom_call" | custom-call | flops 2936012800 | bytes 20000000 | tf_op jit(solution)/shard_map/pallas_call | solution.py:174
  145.7 9.3 %shard_map.187 = bf16[320,3584]{1,0:T(8,128)(2,1)} custom-call(bf16[320,640]{1,0:T(8,128)(2,1)} %get-tuple-element.46.hidden_ref, bf16[4,320,1792]{2,1,0:T(8,128)(2,1)} %bitcast.58, s32[40,3584]{1,0:T(8,128)} %bitcast.72), custom_call_target="tpu_custom_call" | custom-call | flops 2936012800 | bytes 20000000 | tf_op jit(solution)/shard_map/pallas_call | solution.py:218
  155.1 13.5 %collective-permute-done.18 = bf16[256,1152]{1,0:T(8,128)(2,1)S(1)} collective-permute-done((bf16[256,1152]{1,0:T(8,128)(2,1)S(1)}, bf16[256,1152]{1,0:T(8,128)(2,1)S(1)}, u32[]{:S(2)}, u32[]{:S(2)}) %collective-permute-start.18) | collective-permute-done | bytes 589856 | tf_op jit(solution)/shard_map/ppermute | solution.py:290
  169.2 2.4 copy-done.10
  172.7 5.4 %collective-permute-start.6 = (bf16[256,896]{1,0:T(8,128)(2,1)}, bf16[256,896]{1,0:T(8,128)(2,1)}, u32[]{:S(2)}, u32[]{:S(2)}) collective-permute-start(bf16[256,896]{1,0:T(8,128)(2,1)} %dynamic-slice_bitcast_fusion.3), channel_id=1, source_target_pairs={{0,2},{1,3},{2,0},{3,1},{4,6},{5,7},{6,4},{7,5},{8,10},{9,11},{10,... | collective-permute-start | bytes 1376264 | tf_op jit(solution)/shard_map/ppermute | solution.py:285
  179.3 16.9 %shard_map.188 = (bf16[1792,640]{1,0:T(8,128)(2,1)}, bf16[1792,640]{1,0:T(8,128)(2,1)}) custom-call(bf16[4,320,1792]{2,1,0:T(8,128)(2,1)} %bitcast.59, bf16[320,640]{1,0:T(8,128)(2,1)} %get-tuple-element.48.gate_grad_ref, bf16[320,640]{1,0:T(8,128)(2,1)} %get-tuple-element.49.up_grad_ref, s32[224,640]{1,0:T(8,128)} %bitcast.74, s32[224,640]{1,0:T(8,128)} %bitcast.76), custom_call_target="tpu_custom_call" | custom-call | flops 5872025600 | bytes 20000000 | tf_op jit(solution)/shard_map/pallas_call | solution.py:198
  196.2 2.5 constant_dynamic-slice_fusion.3
  207.3 3.2 %constant_dynamic-slice_fusion.steps_ref = bf16[1024,1152]{1,0:T(8,128)(2,1)} fusion(bf16[2048,1152]{1,0:T(8,128)(2,1)} %copy-done.10, s32[]{:T(128)S(6)} %select_n.130), kind=kLoop, calls=%fused_computation.76 | loop fusion | bytes 4718596 | tf_op jit(solution)/shard_map/dynamic_slice | solution.py:309
  210.6 68.9 %collective-permute-done.7 = bf16[128,896]{1,0:T(8,128)(2,1)S(1)} collective-permute-done((bf16[128,896]{1,0:T(8,128)(2,1)S(1)}, bf16[128,896]{1,0:T(8,128)(2,1)S(1)}, u32[]{:S(2)}, u32[]{:S(2)}) %collective-permute-start.7) | collective-permute-done | bytes 229408 | tf_op jit(solution)/shard_map/ppermute | solution.py:285
  280.9 8.4 %shard_map.189 = (bf16[896,384]{1,0:T(8,128)(2,1)}, bf16[896,384]{1,0:T(8,128)(2,1)}, bf16[896,384]{1,0:T(8,128)(2,1)}) custom-call(bf16[1,1024,1792]{2,1,0:T(8,128)(2,1)} %bitcast.60, bf16[1,1024,1792]{2,1,0:T(8,128)(2,1)} %bitcast.61, bf16[1024,1152]{1,0:T(8,128)(2,1)} %constant_dynamic-slice_fusion.steps_ref), custom_call_target="tpu_custom_call" | custom-call | flops 2113929216 | bytes 20000000 | tf_op jit(solution)/shard_map/pallas_call | solution.py:248
  289.3 2.2 add_convert_fusion.3
  291.5 2.7 fusion.2
  294.2 2.6 fusion.3
  296.8 2.5 fusion.4
  (122 shorter events, 28.9 us)
Async XLA Ops:
  7.2 76.4 %all-gather.5.cloned.1.call-start = ((), (), s32[]{:S(2)}) async-start(), calls=%async_computation | async-start | bytes 4128768 | tf_op jit(solution)/shard_map/all_gather | solution.py:372
  9.9 270.9 %all-gather.7.cloned.1.call-start = ((), (), s32[]{:S(2)}) async-start(), calls=%async_computation.1 | async-start | bytes 4128768 | tf_op jit(solution)/shard_map/all_gather | solution.py:409
  14.0 12.4 %collective-permute-start.2 = (bf16[80,1792]{1,0:T(8,128)(2,1)S(1)}, bf16[80,1792]{1,0:T(8,128)(2,1)S(1)}, u32[]{:S(2)}, u32[]{:S(2)}) collective-permute-start(bf16[80,1792]{1,0:T(8,128)(2,1)S(1)} %get-tuple-element.65), channel_id=1, source_target_pairs={{0,12},{4,0},{8,4},{12,8},{1,13},{5,1},{9,5},{13,9},{2,14},{6,2},{... | collective-permute-start | bytes 860168 | tf_op jit(solution)/shard_map/ppermute | solution.py:290
  19.1 24.4 %collective-permute-start.1 = (bf16[80,1792]{1,0:T(8,128)(2,1)S(1)}, bf16[80,1792]{1,0:T(8,128)(2,1)S(1)}, u32[]{:S(2)}, u32[]{:S(2)}) collective-permute-start(bf16[80,1792]{1,0:T(8,128)(2,1)S(1)} %get-tuple-element.66), channel_id=1, source_target_pairs={{0,8},{4,12},{8,0},{12,4},{1,9},{5,13},{9,1},{13,5},{2,10},{6,14},... | collective-permute-start | bytes 860168 | tf_op jit(solution)/shard_map/ppermute | solution.py:290
  19.1 24.4 %collective-permute-start = (bf16[80,1792]{1,0:T(8,128)(2,1)S(1)}, bf16[80,1792]{1,0:T(8,128)(2,1)S(1)}, u32[]{:S(2)}, u32[]{:S(2)}) collective-permute-start(bf16[80,1792]{1,0:T(8,128)(2,1)S(1)} %get-tuple-element.64), channel_id=1, source_target_pairs={{0,4},{4,8},{8,12},{12,0},{1,5},{5,9},{9,13},{13,1},{2,6},{6,10},{... | collective-permute-start | bytes 860168 | tf_op jit(solution)/shard_map/ppermute | solution.py:290
  43.6 27.1 %collective-permute-start.3 = (bf16[320,1792]{1,0:T(8,128)(2,1)S(1)}, bf16[320,1792]{1,0:T(8,128)(2,1)}, u32[]{:S(2)}, u32[]{:S(2)}) collective-permute-start(bf16[320,1792]{1,0:T(8,128)(2,1)S(1)} %pad_maximum_fusion.2), channel_id=1, source_target_pairs={{0,2},{1,3},{2,0},{3,1},{4,6},{5,7},{6,4},{7,5},{8,10},{9,11},{10,... | collective-permute-start | bytes 3440648 | tf_op jit(solution)/shard_map/ppermute | solution.py:285
  74.0 4.8 %collective-permute-start.4 = (bf16[2,320,1792]{2,1,0:T(8,128)(2,1)}, bf16[2,320,1792]{2,1,0:T(8,128)(2,1)}, u32[]{:S(2)}, u32[]{:S(2)}) collective-permute-start(bf16[2,320,1792]{2,1,0:T(8,128)(2,1)} %pad_maximum_fusion.1), channel_id=1, source_target_pairs={{0,1},{1,0},{2,3},{3,2},{4,5},{5,4},{6,7},{7,6},{8,9},{9,8},{10,11... | collective-permute-start | bytes 6881288 | tf_op jit(solution)/shard_map/ppermute | solution.py:285
  74.0 0.7 collective-permute-start.16
  91.3 6.3 %copy-start.3 = (bf16[256,384]{1,0:T(8,128)(2,1)S(1)}, bf16[256,384]{1,0:T(8,128)(2,1)}, u32[]{:S(2)}) copy-start(bf16[256,384]{1,0:T(8,128)(2,1)} %get-tuple-element.53.gate_grad_ref) | copy-start | bytes 589828
  91.3 6.3 %copy-start.2 = (bf16[256,384]{1,0:T(8,128)(2,1)S(1)}, bf16[256,384]{1,0:T(8,128)(2,1)}, u32[]{:S(2)}) copy-start(bf16[256,384]{1,0:T(8,128)(2,1)} %get-tuple-element.54.up_grad_ref) | copy-start | bytes 589828
  91.3 6.4 %copy-start.11 = (bf16[256,384]{1,0:T(8,128)(2,1)S(1)}, bf16[256,384]{1,0:T(8,128)(2,1)}, u32[]{:S(2)}) copy-start(bf16[256,384]{1,0:T(8,128)(2,1)} %get-tuple-element.55) | copy-start | bytes 589828
  97.7 57.3 %collective-permute-start.17 = (bf16[256,1152]{1,0:T(8,128)(2,1)S(1)}, bf16[256,1152]{1,0:T(8,128)(2,1)S(1)}, u32[]{:S(2)}, u32[]{:S(2)}) collective-permute-start(bf16[256,1152]{1,0:T(8,128)(2,1)S(1)} %constant_dynamic-update-slice_fusion.2), channel_id=1, source_target_pairs={{0,12},{4,0},{8,4},{12,8},{1,13},{5,1},{9,5},{13,9},{2,14},{6,2},{... | collective-permute-start | bytes 1769480 | tf_op jit(solution)/shard_map/ppermute | solution.py:290
  114.4 54.2 %collective-permute-start.18 = (bf16[256,1152]{1,0:T(8,128)(2,1)S(1)}, bf16[256,1152]{1,0:T(8,128)(2,1)S(1)}, u32[]{:S(2)}, u32[]{:S(2)}) collective-permute-start(bf16[256,1152]{1,0:T(8,128)(2,1)S(1)} %constant_dynamic-update-slice_fusion.2), channel_id=1, source_target_pairs={{0,8},{4,12},{8,0},{12,4},{1,9},{5,13},{9,1},{13,5},{2,10},{6,14},... | collective-permute-start | bytes 1769480 | tf_op jit(solution)/shard_map/ppermute | solution.py:290
  119.0 49.6 %collective-permute-start.19 = (bf16[256,1152]{1,0:T(8,128)(2,1)S(1)}, bf16[256,1152]{1,0:T(8,128)(2,1)S(1)}, u32[]{:S(2)}, u32[]{:S(2)}) collective-permute-start(bf16[256,1152]{1,0:T(8,128)(2,1)S(1)} %constant_dynamic-update-slice_fusion.2), channel_id=1, source_target_pairs={{0,4},{4,8},{8,12},{12,0},{1,5},{5,9},{9,13},{13,1},{2,6},{6,10},{... | collective-permute-start | bytes 1769480 | tf_op jit(solution)/shard_map/ppermute | solution.py:290
  122.5 49.1 %collective-permute-start.5 = (bf16[2,256,896]{2,1,0:T(8,128)(2,1)S(1)}, bf16[2,256,896]{2,1,0:T(8,128)(2,1)S(1)}, u32[]{:S(2)}, u32[]{:S(2)}) collective-permute-start(bf16[2,256,896]{2,1,0:T(8,128)(2,1)S(1)} %dynamic-slice_bitcast_fusion.1), channel_id=1, source_target_pairs={{0,1},{1,0},{2,3},{3,2},{4,5},{5,4},{6,7},{7,6},{8,9},{9,8},{10,11... | collective-permute-start | bytes 2752520 | tf_op jit(solution)/shard_map/ppermute | solution.py:285
  145.6 32.4 %collective-permute-start.8 = (bf16[2,320,896]{2,1,0:T(8,128)(2,1)S(1)}, bf16[2,320,896]{2,1,0:T(8,128)(2,1)S(1)}, u32[]{:S(2)}, u32[]{:S(2)}) collective-permute-start(bf16[2,320,896]{2,1,0:T(8,128)(2,1)S(1)} %dynamic-slice_bitcast_fusion), channel_id=1, source_target_pairs={{0,1},{1,0},{2,3},{3,2},{4,5},{5,4},{6,7},{7,6},{8,9},{9,8},{10,11... | collective-permute-start | bytes 3440648 | tf_op jit(solution)/shard_map/ppermute | solution.py:285
  169.1 8.9 %copy-start = (bf16[4,320,896]{2,1,0:T(8,128)(2,1)S(1)}, bf16[4,320,896]{2,1,0:T(8,128)(2,1)}, u32[]{:S(2)}) copy-start(bf16[4,320,896]{2,1,0:T(8,128)(2,1)} %shard_map.186) | copy-start | bytes 6881284
  172.7 30.9 %collective-permute-start.6 = (bf16[256,896]{1,0:T(8,128)(2,1)}, bf16[256,896]{1,0:T(8,128)(2,1)}, u32[]{:S(2)}, u32[]{:S(2)}) collective-permute-start(bf16[256,896]{1,0:T(8,128)(2,1)} %dynamic-slice_bitcast_fusion.3), channel_id=1, source_target_pairs={{0,2},{1,3},{2,0},{3,1},{4,6},{5,7},{6,4},{7,5},{8,10},{9,11},{10,... | collective-permute-start | bytes 1376264 | tf_op jit(solution)/shard_map/ppermute | solution.py:285
  179.2 26.1 %collective-permute-start.9 = (bf16[320,896]{1,0:T(8,128)(2,1)}, bf16[320,896]{1,0:T(8,128)(2,1)}, u32[]{:S(2)}, u32[]{:S(2)}) collective-permute-start(bf16[320,896]{1,0:T(8,128)(2,1)} %dynamic-slice_bitcast_fusion.2), channel_id=1, source_target_pairs={{0,2},{1,3},{2,0},{3,1},{4,6},{5,7},{6,4},{7,5},{8,10},{9,11},{10,... | collective-permute-start | bytes 1720328 | tf_op jit(solution)/shard_map/ppermute | solution.py:285
  196.2 5.7 %copy-start.6 = (bf16[320,3584]{1,0:T(8,128)(2,1)S(1)}, bf16[320,3584]{1,0:T(8,128)(2,1)}, u32[]{:S(2)}) copy-start(bf16[320,3584]{1,0:T(8,128)(2,1)} %shard_map.187) | copy-start | bytes 6881284
  198.7 92.7 %collective-permute-start.13 = (bf16[896,640]{1,0:T(8,128)(2,1)}, bf16[896,640]{1,0:T(8,128)(2,1)}, u32[]{:S(2)}, u32[]{:S(2)}) collective-permute-start(bf16[896,640]{1,0:T(8,128)(2,1)} %constant_dynamic-slice_fusion.3), channel_id=1, source_target_pairs={{0,16},{16,0},{1,17},{17,1},{2,18},{18,2},{3,19},{19,3},{4,20},{20... | collective-permute-start | bytes 3440648 | tf_op jit(solution)/shard_map/ppermute | solution.py:285
  201.4 92.8 %collective-permute-start.14 = (bf16[896,640]{1,0:T(8,128)(2,1)}, bf16[896,640]{1,0:T(8,128)(2,1)}, u32[]{:S(2)}, u32[]{:S(2)}) collective-permute-start(bf16[896,640]{1,0:T(8,128)(2,1)} %constant_dynamic-slice_fusion.2), channel_id=1, source_target_pairs={{0,16},{16,0},{1,17},{17,1},{2,18},{18,2},{3,19},{19,3},{4,20},{20... | collective-permute-start | bytes 3440648 | tf_op jit(solution)/shard_map/ppermute | solution.py:285
  202.0 94.8 %collective-permute-start.15 = (bf16[320,1792]{1,0:T(8,128)(2,1)S(1)}, bf16[320,1792]{1,0:T(8,128)(2,1)}, u32[]{:S(2)}, u32[]{:S(2)}) collective-permute-start(bf16[320,1792]{1,0:T(8,128)(2,1)S(1)} %constant_dynamic-slice_fusion.1), channel_id=1, source_target_pairs={{0,16},{16,0},{1,17},{17,1},{2,18},{18,2},{3,19},{19,3},{4,20},{20... | collective-permute-start | bytes 3440648 | tf_op jit(solution)/shard_map/ppermute | solution.py:285
  204.7 5.9 %copy-start.12 = (bf16[256,896]{1,0:T(8,128)(2,1)}, bf16[256,896]{1,0:T(8,128)(2,1)S(1)}, u32[]{:S(2)}) copy-start(bf16[256,896]{1,0:T(8,128)(2,1)S(1)} %fusion.7) | copy-start | bytes 1376260
  204.7 74.7 %collective-permute-start.7 = (bf16[128,896]{1,0:T(8,128)(2,1)S(1)}, bf16[128,896]{1,0:T(8,128)(2,1)S(1)}, u32[]{:S(2)}, u32[]{:S(2)}) collective-permute-start(bf16[128,896]{1,0:T(8,128)(2,1)S(1)} %constant_dynamic-slice_fusion.4), channel_id=1, source_target_pairs={{0,16},{16,0},{1,17},{17,1},{2,18},{18,2},{3,19},{19,3},{4,20},{20... | collective-permute-start | bytes 688136 | tf_op jit(solution)/shard_map/ppermute | solution.py:285
  207.3 72.2 %collective-permute-start.12 = (bf16[80,896]{1,0:T(8,128)(2,1)S(1)}, bf16[80,896]{1,0:T(8,128)(2,1)S(1)}, u32[]{:S(2)}, u32[]{:S(2)}) collective-permute-start(bf16[80,896]{1,0:T(8,128)(2,1)S(1)} %get-tuple-element.68), channel_id=1, source_target_pairs={{0,4},{4,8},{8,12},{12,0},{1,5},{5,9},{9,13},{13,1},{2,6},{6,10},{... | collective-permute-start | bytes 430088 | tf_op jit(solution)/shard_map/ppermute | solution.py:290
  279.5 9.8 %collective-permute-start.11 = (bf16[80,896]{1,0:T(8,128)(2,1)}, bf16[80,896]{1,0:T(8,128)(2,1)}, u32[]{:S(2)}, u32[]{:S(2)}) collective-permute-start(bf16[80,896]{1,0:T(8,128)(2,1)} %get-tuple-element.69), channel_id=1, source_target_pairs={{0,8},{4,12},{8,0},{12,4},{1,9},{5,13},{9,1},{13,5},{2,10},{6,14},... | collective-permute-start | bytes 430088 | tf_op jit(solution)/shard_map/ppermute | solution.py:290
  280.8 8.4 %collective-permute-start.10 = (bf16[80,896]{1,0:T(8,128)(2,1)}, bf16[80,896]{1,0:T(8,128)(2,1)}, u32[]{:S(2)}, u32[]{:S(2)}) collective-permute-start(bf16[80,896]{1,0:T(8,128)(2,1)} %get-tuple-element.70), channel_id=1, source_target_pairs={{0,12},{4,0},{8,4},{12,8},{1,13},{5,1},{9,5},{13,9},{2,14},{6,2},{... | collective-permute-start | bytes 430088 | tf_op jit(solution)/shard_map/ppermute | solution.py:290
  280.8 8.4 %copy-start.13 = (bf16[256,896]{1,0:T(8,128)(2,1)S(1)}, bf16[256,896]{1,0:T(8,128)(2,1)}, u32[]{:S(2)}) copy-start(bf16[256,896]{1,0:T(8,128)(2,1)} %copy-done.12) | copy-start | bytes 1376260
  280.8 8.4 %copy-start.15 = (bf16[80,896]{1,0:T(8,128)(2,1)S(1)}, bf16[80,896]{1,0:T(8,128)(2,1)}, u32[]{:S(2)}) copy-start(bf16[80,896]{1,0:T(8,128)(2,1)} %get-tuple-element.67) | copy-start | bytes 430084
  280.8 8.4 %copy-start.18 = (bf16[128,896]{1,0:T(8,128)(2,1)S(1)}, bf16[128,896]{1,0:T(8,128)(2,1)}, u32[]{:S(2)}) copy-start(bf16[128,896]{1,0:T(8,128)(2,1)} %copy-done.17) | copy-start | bytes 688132
  280.8 8.4 %copy-start.20 = (bf16[80,896]{1,0:T(8,128)(2,1)S(1)}, bf16[80,896]{1,0:T(8,128)(2,1)}, u32[]{:S(2)}) copy-start(bf16[80,896]{1,0:T(8,128)(2,1)} %copy-done.19) | copy-start | bytes 430084
  (11 other events, 23.2 us)
Sparse Core Ops, SparseCore 0:
  10.5 37.7 all-gather.4
  75.6 59.3 all-gather.6
